TPU v7x, 256 devices: a whole 4x4x8 slice. The times are simulated.
256 devices in a mesh: chan: 32 (over z, y_lo, core), bin: 8 (over y_hi, x).
Axes of the slice: x: 4, y: 4 (y_hi: 2, y_lo: 2; y = y_hi * 2 + y_lo), z: 8, core: 2. Of those that a mesh axis runs over, the one named last changes fastest.
Arguments:
- traces: float32 [6144, 4096], P(('chan', 'bin')), may hold values from -6 to 6
- fir_taps: float32 [64], replicated, may hold values from -0.75 to 0.75
- pair_bin: int32 [6144, 6144], P(('chan', 'bin')), may hold values from 0 to 63, as said below
Outputs:
- stacks: float32 [64, 512], P('bin')
Inputs may be any that keep to these rules, and one draw needn't show every extreme that they name: pair_bin[a, b] equals pair_bin[b, a].
All inputs are finite; a program needn't handle non-finite values.
Results may differ from a plain program's by a relative error of at most 0.0051.
Values may be sent and summed in bfloat16 or wider, within the bound.
A program may use at most 320 MiB of HBM per device.

v0:
```python
import math

import jax
import jax.numpy as jnp
from jax import lax
from jax.sharding import PartitionSpec as P

SAMPLES = 4096
TAPS = 64
BAND_LO = 64
NF = 192
MARGIN = 32
LAGS = 512
NBINS = 64


def whiten(traces, fir_taps):
    filtered = jnp.zeros_like(traces)
    for shift_count in range(TAPS):
        moved = jnp.pad(traces[:, : SAMPLES - shift_count], ((0, 0), (shift_count, 0)))
        filtered = filtered + fir_taps[shift_count] * moved
    width = NF + 2 * MARGIN
    times = jnp.arange(SAMPLES, dtype=jnp.int32)
    freqs = BAND_LO - MARGIN + jnp.arange(width, dtype=jnp.int32)
    phase = times[:, None] * freqs[None, :] % SAMPLES
    angle = 2.0 * math.pi / SAMPLES * phase.astype(jnp.float32)
    ext_re = jnp.dot(filtered, jnp.cos(angle), precision=lax.Precision.HIGHEST)
    ext_im = -jnp.dot(filtered, jnp.sin(angle), precision=lax.Precision.HIGHEST)
    power = ext_re * ext_re + ext_im * ext_im
    source = jnp.arange(width, dtype=jnp.int32)[:, None]
    target = jnp.arange(NF, dtype=jnp.int32)[None, :]
    window = ((source >= target) & (source < target + 2 * MARGIN)).astype(jnp.float32)
    smooth = jnp.dot(power, window, precision=lax.Precision.HIGHEST) / (2.0 * MARGIN)
    scale = 1.0 / jnp.sqrt(smooth + 1e-06)
    band_re = ext_re[:, MARGIN : MARGIN + NF] * scale
    band_im = ext_im[:, MARGIN : MARGIN + NF] * scale
    return jnp.concatenate([band_re, band_im], axis=1).astype(jnp.bfloat16)


def lag_table():
    freq = BAND_LO + jnp.arange(NF, dtype=jnp.int32)
    lag = jnp.arange(LAGS, dtype=jnp.int32) - LAGS // 2
    phase = freq[:, None] * lag[None, :] % SAMPLES
    angle = 2.0 * math.pi / SAMPLES * phase.astype(jnp.float32)
    return jnp.concatenate([jnp.cos(angle), -jnp.sin(angle)], axis=0) * (2.0 / SAMPLES)


def stack_block(local, piece, rows_bins, include, sign):
    left = local.astype(jnp.float32)
    right = piece.astype(jnp.float32)
    ar, ai = (left[:, :NF], left[:, NF:])
    br, bi = (right[:, :NF], right[:, NF:])
    real_part = ar[:, None, :] * br[None, :, :] + ai[:, None, :] * bi[None, :, :]
    imag_part = (ai[:, None, :] * br[None, :, :] - ar[:, None, :] * bi[None, :, :]) * sign[
        :, :, None
    ]
    pairs = local.shape[0] * piece.shape[0]
    cross = (
        jnp.concatenate([real_part, imag_part], axis=2).astype(jnp.bfloat16).reshape(pairs, 2 * NF)
    )
    codes = jnp.arange(NBINS, dtype=jnp.int32)
    onehot = (
        ((rows_bins[:, :, None] == codes[None, None, :]) & include[:, :, None])
        .astype(jnp.bfloat16)
        .reshape(pairs, NBINS)
    )
    return lax.dot_general(
        onehot, cross, (((0,), (0,)), ((), ())), preferred_element_type=jnp.float32
    )


def per_device(traces, fir_taps, pair_bin):
    white = whiten(traces, fir_taps)
    group = lax.all_gather(white, "bin", axis=0, tiled=True)
    n_bin = lax.axis_size("bin")
    my_group = lax.axis_index("chan")
    my_place = lax.axis_index("bin")
    rows = traces.shape[0]
    own_index = (my_group * n_bin + my_place) * rows + jnp.arange(rows, dtype=jnp.int32)
    piece = lax.all_gather(group, "chan", axis=0, tiled=True)
    width = piece.shape[0]
    other_index = jnp.arange(width, dtype=jnp.int32)
    include = own_index[:, None] < other_index[None, :]
    sign = jnp.ones((rows, width), jnp.float32)
    partial_stack = stack_block(white, piece, pair_bin, include, sign)
    owned = lax.psum_scatter(partial_stack, "bin", scatter_dimension=0, tiled=True)
    total = lax.psum(owned, "chan")
    return jnp.dot(total, lag_table(), precision=lax.Precision.HIGHEST)


def solution(mesh):
    return jax.shard_map(
        per_device,
        mesh=mesh,
        in_specs=(P(("chan", "bin"), None), P(), P(("chan", "bin"), None)),
        out_specs=P("bin", None),
        check_vma=False,
    )
```

profile of v0, /device:TPU:1, one launch (start us, length us, event | category | flops | bytes accessed | tf_op | source)
XLA Modules:
  0.0 540.8 jit_solution(5566907273677622713)
XLA Ops:
  6.5 0.0 all-gather.2.cloned.1.call-start
  6.5 2.1 fusion.57
  8.6 2.1 fusion.58
  10.7 2.1 fusion.59
  12.8 1.6 fusion.60
  14.3 61.3 %multiply_add_fusion = f32[24,4096]{1,0:T(8,128)S(1)} fusion(f32[24,4033]{1,0:T(8,128)} %bitcast.134, f32[24,4034]{1,0:T(8,128)} %bitcast.135, f32[24,4035]{1,0:T(8,128)} %bitcast.136, f32[24,4036]{1,0:T(8,128)} %bitcast.137, f32[24,4037]{1,0:T(8,128)} %bitcast.138, f32[24,4038]{1,0:T(8,128)} %bitcast.139, f32[24,4039]{1,0:T(8,128)} %bitcast.140, ...), kind=kLoop, calls=%fused_computation.44 | loop fusion | flops 12484608 | bytes 25365760 | tf_op jit(solution)/shard_map/add | solution.py:21
  75.6 17.3 %fusion.11 = f32[24,256]{1,0:T(8,128)S(1)} fusion(f32[24,4096]{1,0:T(8,128)S(1)} %multiply_add_fusion, s32[256]{0:T(256)S(1)} %iota_add_fusion.2), kind=kOutput, calls=%fused_computation.16 | convolution fusion | flops 316669952 | bytes 418816 | tf_op jit(solution)/shard_map/dot_general | solution.py:28
  93.0 17.4 %fusion.13 = f32[24,256]{1,0:T(8,128)S(1)} fusion(f32[24,4096]{1,0:T(8,128)S(1)} %multiply_add_fusion, s32[256]{0:T(256)S(1)} %iota_add_fusion.2), kind=kOutput, calls=%fused_computation.18 | convolution fusion | flops 316669952 | bytes 418816 | tf_op jit(solution)/shard_map/dot_general | solution.py:27
  110.4 0.2 fusion.40
  110.6 0.1 pad_maximum_fusion
  110.7 31.4 %all_gather.6 = bf16[192,384]{1,0:T(8,128)(2,1)} all-gather(bf16[24,384]{1,0:T(8,128)(2,1)S(1)} %pad_maximum_fusion), channel_id=1, replica_groups=mesh['chan'=32,'bin'=8] {'bin'}, dimensions={0}, use_global_device_ids=true | all-gather | bytes 165888 | tf_op jit(solution)/shard_map/all_gather | solution.py:74
  142.1 0.0 all-gather.2.cloned.1.call-update
  142.1 0.0 all-reduce.66.cloned.1.call-start
  142.2 0.1 fusion.56
  142.3 0.1 iota_compare_fusion.1
  142.5 76.8 %all-gather.2.cloned.1.call-done = bf16[6144,384]{1,0:T(8,128)(2,1)} async-done(((bf16[192,384]{1,0:T(8,128)(2,1)}), bf16[6144,384]{1,0:T(8,128)(2,1)}) %all-gather.2.cloned.1.call-update) | async-done | bytes 4718608 | tf_op jit(solution)/shard_map/all_gather | solution.py:80
  219.2 8.6 %fusion.55 = (f32[6144,192]{1,0:T(8,128)}, f32[6144,192]{1,0:T(8,128)}) fusion(bf16[6144,384]{1,0:T(8,128)(2,1)} %all-gather.2.cloned.1.call-done), kind=kLoop, calls=%fused_computation.73 | loop fusion | bytes 18874368 | tf_op jit(solution)/shard_map/slice | solution.py:52
  227.8 0.0 copy-start
  227.8 59.5 %add_convert_fusion = (bf16[24,6144,192]{2,1,0:T(8,128)(2,1)}, bf16[24,6144,192]{2,1,0:T(8,128)(2,1)}) fusion(f32[6144,192]{1,0:T(8,128)} %get-tuple-element.8, f32[24,192]{1,0:T(8,128)S(1)} %get-tuple-element.12, f32[6144,192]{1,0:T(8,128)} %get-tuple-element.7, f32[24,192]{1,0:T(8,128)S(1)} %get-tuple-element.11), kind=kLoop, calls=%fused_computation.1 | loop fusion | flops 226492416 | bytes 122720256 | tf_op jit(solution)/shard_map/convert
  287.3 0.0 copy-done
  287.3 0.0 copy-start.1
  287.3 59.1 %fusion.20 = f32[64,384]{1,0:T(8,128)} fusion(bf16[24,6144,192]{2,1,0:T(8,128)(2,1)} %get-tuple-element.6, bf16[24,6144,192]{2,1,0:T(8,128)(2,1)} %get-tuple-element.5, s32[24,6144]{1,0:T(8,128)S(1)} %copy-done, pred[24,6144]{1,0:T(8,128)(4,1)S(1)} %iota_compare_fusion.1), kind=kOutput, calls=%fused_computation.23 | convolution fusion | flops 7493124096 | bytes 114081792 | tf_op jit(solution)/shard_map/dot_general | solution.py:67
  346.5 0.0 all-reduce.66.cloned.1.call-update
  346.5 1.6 fusion.36
  348.1 0.0 copy-done.1
  348.1 0.6 dynamic-slice
  349.4 77.1 %all-reduce.66.cloned.1.call-done = f32[64,384]{1,0:T(8,128)} async-done(((f32[64,384]{1,0:T(8,128)}), f32[64,384]{1,0:T(8,128)}) %all-reduce.66.cloned.1.call-update) | async-done | bytes 98320
  426.4 0.7 constant_dynamic-slice_fusion
  427.2 105.5 %psum.7 = f32[8,384]{1,0:T(8,128)S(1)} all-reduce(f32[8,384]{1,0:T(8,128)S(1)} %constant_dynamic-slice_fusion), channel_id=1, replica_groups=mesh['chan'=32,'bin'=8] {'chan'}, use_global_device_ids=true, to_apply=%region_1.2 | all-reduce | flops 3072 | bytes 24576 | tf_op jit(solution)/shard_map/psum | solution.py:87
  532.7 1.1 fusion.27
  (4 shorter events, 0.0 us)
Async XLA Ops:
  6.5 212.7 %all-gather.2.cloned.1.call-start = ((), (), s32[]{:S(2)}) async-start(), calls=%async_computation | async-start | bytes 4866048 | tf_op jit(solution)/shard_map/all_gather | solution.py:80
  142.1 284.3 %all-reduce.66.cloned.1.call-start = ((), (), s32[]{:S(2)}) async-start(), calls=%async_computation.1 | async-start | bytes 196608
  227.8 59.5 %copy-start = (s32[24,6144]{1,0:T(8,128)S(1)}, s32[24,6144]{1,0:T(8,128)}, u32[]{:S(2)}) copy-start(s32[24,6144]{1,0:T(8,128)} %param.5) | copy-start | bytes 1769476
  287.3 60.8 %copy-start.1 = (u32[256]{0:T(256)S(1)}, u32[256]{0:T(256)}, u32[]{:S(2)}) copy-start(u32[256]{0:T(256)} %constant.188) | copy-start | bytes 3076
Sparse Core Ops, SparseCore 0:
  142.3 76.9 all-gather.1
  346.6 79.7 all-reduce.65
where the time goes:
time: 547 us; the launch traced here: 541 us
  waiting for transfers between devices  154 us (28%)
  blocking collectives  137 us (25%)
  other arithmetic  123 us (22%)
  matrix products  95.2 us (17%)
  local copies, waits for them, and re-layouts  17.7 us (3%)
  between operations  14.4 us (3%)
    psum x1, blocking collectives, per_device(): total = lax.psum(owned, 'chan')  106 us
    unnamed x3, waiting for transfers between devices  77.1 us
    all_gather x1, waiting for transfers between devices, per_device(): piece = lax.all_gather(group, 'chan', axis=0, tiled=True)  76.8 us
    add x1, other arithmetic, whiten(): filtered = filtered + fir_taps[shift_count] * moved  61.3 us
    another operation x1, other arithmetic  59.5 us
    dot_general x1, matrix products, stack_block(): lax.dot_general(onehot, cross, (((0,), (0,)), ((), ())), preferred_elemen...  59.1 us
    all_gather x1, blocking collectives, per_device(): group = lax.all_gather(white, 'bin', axis=0, tiled=True)  31.4 us
    dot_general x1, matrix products, whiten(): ext_re = jnp.dot(filtered, jnp.cos(angle), precision=lax.Precision.HIGHEST)  17.4 us
  transfers between devices with their start and end apart: 2, of which 2 were waited for; matrix products, arithmetic and copies ran while one was open for 0% of the time, Pallas kernels for 0%

commit v1 on v0

v1 whole, which is shorter than its diff:
```python
import math

import jax
import jax.numpy as jnp
import ml_dtypes
import numpy as np
from jax import lax
from jax.experimental import pallas as pl
from jax.experimental.pallas import tpu as pltpu
from jax.sharding import PartitionSpec as P

SAMPLES = 4096
TAPS = 64
BAND_LO = 64
NF = 192
MARGIN = 32
LAGS = 512
NBINS = 64
ROWS = 24
LEVEL = 768
MESH = pl.DeviceIdType.MESH
F32 = jnp.float32
BF16 = jnp.bfloat16


def lane_freqs():
    lane = np.arange(128)
    return np.concatenate([16 * (lane % 16) + 8 * j + lane // 16 for j in range(2)])


def split2(table):
    hi = table.astype(ml_dtypes.bfloat16)
    lo = (table - hi.astype(np.float64)).astype(ml_dtypes.bfloat16)
    return hi, lo


def make_tables():
    e = lane_freqs()
    u = np.arange(256)
    ang = 2 * math.pi / SAMPLES * ((u[None, :] * np.arange(16)[:, None]) % SAMPLES)
    twiddle = np.concatenate([np.cos(ang), np.sin(ang)], 0).astype(np.float32)
    p = 2 + np.arange(128) % 16
    ang = 2 * math.pi / 256 * ((u[:, None] * p[None, :]) % 256)
    c, s = np.cos(ang), np.sin(ang)
    fine = np.concatenate([np.concatenate([c, -s], 1), np.concatenate([s, c], 1)], 0)
    ang = 2 * math.pi / SAMPLES * ((np.arange(128)[:, None] * (32 + e)[None, :]) % SAMPLES)
    taps = np.concatenate([np.cos(ang), -np.sin(ang)], 1)
    taps[TAPS:] = 0.0
    window = ((e[:, None] >= e[None, :] - MARGIN) & (e[:, None] < e[None, :] + MARGIN)) / (2.0 * MARGIN)
    f = e - MARGIN
    ok = (f >= 0) & (f < NF)
    phase = ((BAND_LO + np.where(ok, f, 0))[:, None] * (np.arange(LAGS) - LAGS // 2)[None, :]) % SAMPLES
    ang = 2 * math.pi / SAMPLES * phase
    lag = np.concatenate([np.cos(ang), -np.sin(ang)], 0) * (2.0 / SAMPLES) * np.concatenate([ok, ok])[:, None]
    return (twiddle, *split2(fine), taps.astype(np.float32), window.astype(ml_dtypes.bfloat16), *split2(lag))


def dot(a, b, **kw):
    return jnp.dot(a, b, preferred_element_type=F32, **kw)


def halves(a):
    hi = a.astype(BF16)
    return hi, (a - hi.astype(F32)).astype(BF16)


def sixteen(x):
    root = math.sqrt(0.5)
    a = [x[k] + x[k + 8] for k in range(8)]
    b = [x[k] - x[k + 8] for k in range(8)]
    c = [a[k] + a[k + 4] for k in range(4)]
    d = [a[k] - a[k + 4] for k in range(4)]
    y = [None] * 9
    zero = jnp.zeros_like(x[0])
    even, odd = c[0] + c[2], c[1] + c[3]
    y[0] = (even + odd, zero)
    y[8] = (even - odd, zero)
    y[4] = (c[0] - c[2], c[3] - c[1])
    m, n = (d[1] - d[3]) * root, (d[1] + d[3]) * root
    y[2] = (d[0] + m, -(n + d[2]))
    y[6] = (d[0] - m, d[2] - n)
    for r in (1, 3, 5, 7):
        re, im = b[0], b[4] * (-1.0 if r % 4 == 1 else 1.0)
        for k in (1, 2, 3):
            re = re + (b[k] - b[8 - k]) * math.cos(math.pi * k * r / 8)
            im = im - (b[k] + b[8 - k]) * math.sin(math.pi * k * r / 8)
        y[r] = (re, im)
    return y


def whiten(x_ref, taps, tw_ref, fine_hi, fine_lo, tap_table, window, t_ref):
    for i in range(3):
        for j in range(2):
            rows, lanes = pl.ds(8 * i, 8), pl.ds(128 * j, 128)
            y = sixteen([x_ref[rows, pl.ds(256 * w + 128 * j, 128)] for w in range(16)])
            for r in range(16):
                re, im = y[min(r, 16 - r)]
                if r > 8:
                    im = -im
                if r:
                    c, s = tw_ref[pl.ds(r, 1), lanes], tw_ref[pl.ds(16 + r, 1), lanes]
                    re, im = re * c + im * s, im * c - re * s
                t_ref[pl.ds(24 * r + 8 * i, 8), lanes] = re
                t_ref[pl.ds(24 * r + 8 * i, 8), pl.ds(256 + 128 * j, 128)] = im
    hi, lo = halves(t_ref[...])
    fine = fine_hi[...]
    z = dot(hi, fine) + dot(lo, fine) + dot(hi, fine_lo[...])
    lane = lax.broadcasted_iota(jnp.int32, (24, 128), 1)
    ext = []
    for part in range(2):
        for j in range(2):
            tile = jnp.zeros((24, 128), F32)
            for r in range(8):
                piece = z[24 * (8 * j + r) : 24 * (8 * j + r) + 24, 128 * part : 128 * part + 128]
                tile = jnp.where(lane // 16 == r, piece, tile)
            ext.append(tile)
    padded = jnp.concatenate([taps, jnp.zeros((1, 64), F32)], axis=1)
    shifted = pltpu.roll(jnp.broadcast_to(padded, (128, 128)), 0, 1, stride=1, stride_axis=0)
    gains = dot(shifted, tap_table[...], precision=lax.Precision.HIGHEST)
    last = jnp.where(lane >= 64, x_ref[:, pl.ds(SAMPLES - 128, 128)], 0.0)
    cut = dot(last, gains, precision=lax.Precision.HIGHEST)
    h = [gains[0:1, 128 * k : 128 * k + 128] for k in range(4)]
    re = [h[j] * ext[j] - h[2 + j] * ext[2 + j] - cut[:, 128 * j : 128 * j + 128] for j in range(2)]
    im = [h[j] * ext[2 + j] + h[2 + j] * ext[j] - cut[:, 256 + 128 * j : 384 + 128 * j] for j in range(2)]
    power = jnp.concatenate([re[j] * re[j] + im[j] * im[j] for j in range(2)], axis=1)
    one = power.astype(BF16)
    rest = power - one.astype(F32)
    two = rest.astype(BF16)
    three = (rest - two.astype(F32)).astype(BF16)
    win = window[...]
    smooth = dot(one, win) + dot(two, win) + dot(three, win)
    scale = 1.0 / jnp.sqrt(smooth + 1e-06)
    r0, r1 = (re[j] * scale[:, 128 * j : 128 * j + 128] for j in range(2))
    i0, i1 = (im[j] * scale[:, 128 * j : 128 * j + 128] for j in range(2))
    slot = lane % 16
    band = (slot >= 2) & (slot < 14)

    def pack(a, b, c, d):
        return [
            jnp.where(band, t, pltpu.roll(d, s, 1)) for t, s in ((a, 12), (b, 8), (c, 4))
        ]

    return pack(r0, r1, i0, i1), pack(i0, i1, r0, r1)


def unpack(tiles, rows):
    slot = lax.broadcasted_iota(jnp.int32, (rows, 128), 1) % 16
    a, b, c = (pltpu.roll(t, s, 1) for t, s in zip(tiles, (116, 120, 124)))
    return jnp.where(slot < 6, a, jnp.where(slot < 10, b, c))


def mod(a, n):
    return lax.rem(a, jnp.int32(n))


def kernel(
    x_hbm, taps_ref, bins_hbm, tw_hbm, fhi_hbm, flo_hbm, tap_hbm, win_hbm, lhi_hbm, llo_hbm,
    out_ref,
    x_ref, tw_ref, fhi_ref, flo_ref, tap_ref, win_ref, lhi_ref, llo_ref, lev_ref, t_ref,
    zbuf, abuf, own_a, tiles, sib_tiles, wa_ref, hot, gath, x_acc, y_acc, part, r1, r2, r3,
    in_sem, lev_sem, z_send, z_recv, s_send, s_recv, p1_send, p1_recv, p2_send, p2_recv,
    r1_send, r1_recv, r2_send, r2_recv, r3_send, r3_recv,
):
    chan, place = lax.axis_index("chan"), lax.axis_index("bin")
    z, quad = lax.div(chan, jnp.int32(4)), mod(chan, 4)
    y_lo, core = lax.div(quad, jnp.int32(2)), mod(quad, 2)
    y_hi, x = lax.div(place, jnp.int32(4)), mod(place, 4)
    y = 2 * y_hi + y_lo
    upper = lax.div(z, jnp.int32(4))
    c = z + upper * (11 - 2 * z)
    me = 16 * y_lo + 8 * core + place

    def z_of(pos):
        return pos + lax.div(pos, jnp.int32(4)) * (11 - 2 * pos)

    def device(xx, yy, zz, cc):
        return (4 * zz + 2 * mod(yy, 2) + cc, 4 * lax.div(yy, jnp.int32(2)) + xx)

    loads = [
        pltpu.make_async_copy(src, dst, in_sem.at[i])
        for i, (src, dst) in enumerate(
            (
                (x_hbm, x_ref), (tw_hbm, tw_ref), (fhi_hbm, fhi_ref), (flo_hbm, flo_ref),
                (tap_hbm, tap_ref), (win_hbm, win_ref), (lhi_hbm, lhi_ref), (llo_hbm, llo_ref),
            )
        )
    ]
    for load in loads[:6]:
        load.start()
    levels = [z_of(mod(c + i, 8)) for i in range(5)]
    lev_loads = [
        pltpu.make_async_copy(
            bins_hbm.at[:, pl.ds(pl.multiple_of(levels[i] * LEVEL, 128), LEVEL)], lev_ref.at[i], lev_sem.at[i]
        )
        for i in range(5)
    ]
    for load in lev_loads:
        load.start()
    for load in loads[6:]:
        load.start()

    friends = [device(x, y, mod(z + d, 8), core) for d in range(1, 8)]
    friends += [device(mod(x + d, 4), y, z, core) for d in range(1, 4)]
    friends += [device(x, mod(y + d, 4), z, core) for d in range(1, 4)]
    friends += [device(mod(x + d, 4), mod(y + 2, 4), z, core) for d in range(1, 4)]
    other_quad = [mod(quad + d, 4) for d in range(1, 4)]
    pairs = [(4 * z + q, place) for q in other_quad]
    sibling = (chan + 1 - 2 * core, place)
    across = y + 1 - 2 * y_lo
    friends += [sibling, device(x, across, z, 1 - core)]
    barrier = pltpu.get_barrier_semaphore()
    for friend in friends:
        pl.semaphore_signal(barrier, inc=1, device_id=friend, device_id_type=MESH)

    def remote(src, dst, send, recv, to):
        return pltpu.make_async_remote_copy(
            src_ref=src, dst_ref=dst, send_sem=send, recv_sem=recv, device_id=to, device_id_type=MESH
        )

    for load in loads[:6]:
        load.wait()
    white, swapped = whiten(x_ref, taps_ref[...], tw_ref, fhi_ref, flo_ref, tap_ref, win_ref, t_ref)
    pad = jnp.zeros((8, 128), F32)
    for t in range(3):
        lanes = pl.ds(128 * t, 128)
        first = jnp.concatenate([white[t], pad], axis=0).astype(BF16)
        second = jnp.concatenate([swapped[t], pad], axis=0).astype(BF16)
        zbuf[0, :, lanes] = first
        own_a[0, :, lanes] = first
        own_a[1, :, lanes] = second
    pl.semaphore_wait(barrier, len(friends))

    sends = []

    def go(copy):
        copy.start()
        sends.append(copy)
        return copy

    z_copies = [
        go(remote(zbuf.at[0], zbuf.at[i], z_send.at[i - 1], z_recv.at[i - 1], device(x, y, z_of(mod(c + 8 - i, 8)), core)))
        for i in range(1, 5)
    ]
    a_copy = go(remote(own_a, abuf, s_send.at[0], s_recv.at[0], sibling))

    for load in lev_loads:
        load.wait()
    row = lax.broadcasted_iota(jnp.int32, (24, LEVEL), 0)
    col = lax.broadcasted_iota(jnp.int32, (24, LEVEL), 1)
    sign = 1 - 2 * upper
    after = (col - (24 * me + row)) * sign > 0
    lev_ref[0] = jnp.where(after, lev_ref[0], -1)
    half = (col >= LEVEL // 2).astype(jnp.int32)
    lev_ref[4] = jnp.where(mod(half + y_lo + upper, 2) == 0, lev_ref[4], -1)
    lane = lax.broadcasted_iota(jnp.int32, (24, 128), 1)
    for g in range(32):
        tile = jnp.full((24, 128), -1.0, F32)
        t0, off = divmod(24 * g, 128)
        for i in range(5):
            shift = (24 * i - off) % 128
            piece = pltpu.roll(lev_ref[i, :, pl.ds(128 * t0, 128)].astype(F32), shift, 1)
            if off > 104:
                more = pltpu.roll(lev_ref[i, :, pl.ds(128 * t0 + 128, 128)].astype(F32), shift, 1)
                piece = jnp.where(lane < 24 * i + 128 - off, piece, more)
            tile = jnp.where((lane >= 24 * i) & (lane < 24 * i + 24), piece, tile)
        tiles[g // 8 % 2, 8 * (g // 16) + g % 8] = tile
    b_copy = go(remote(tiles.at[1 - core], sib_tiles, s_send.at[1], s_recv.at[1], sibling))

    codes = lax.broadcasted_iota(jnp.int32, (64, 128), 0).astype(F32).astype(BF16)

    def place_of(d2, d1):
        xx = mod(x + core * d2 + (1 - core) * d1, 4)
        yy = mod(y + core * d1 + (1 - core) * d2, 4)
        return 8 * mod(yy, 2) + 4 * lax.div(yy, jnp.int32(2)) + xx

    def one_hots(source, base):
        def body(j, carry):
            at = place_of(lax.div(j, jnp.int32(4)), mod(j, 4))
            lanes = pl.ds(pl.multiple_of(128 * j, 128), 128)
            for a in range(24):
                bins = jnp.broadcast_to(source(at, a), (16, 128)).astype(BF16)
                for k in range(4):
                    hot[pl.ds(base + 64 * a + 16 * k, 16), lanes] = jnp.where(
                        bins == codes[16 * k : 16 * k + 16], jnp.ones((), BF16), jnp.zeros((), BF16)
                    )
            return carry

        lax.fori_loop(0, 16, body, 0)

    one_hots(lambda at, a: tiles[core, at, pl.ds(a, 1), :], 0)

    for copy in z_copies:
        copy.wait_recv()
    blocks = [zbuf[i, pl.ds(0, 32), :].astype(F32)[:24] for i in range(5)]
    gath[0, 0] = jnp.concatenate(blocks + [jnp.zeros((8, 384), F32)], axis=0).astype(BF16)

    def first(d):
        return device(mod(x + (1 - core) * d, 4), mod(y + core * d, 4), z, core)

    def second(d):
        return device(mod(x + core * d, 4), mod(y + (1 - core) * d, 4), z, core)

    order = (1, 3, 2)
    p1 = [go(remote(gath.at[0, 0], gath.at[0, 4 - d], p1_send.at[n], p1_recv.at[n], first(d))) for n, d in enumerate(order)]
    p2 = {}

    def forward(d1):
        for n, d in enumerate(order):
            p2[4 - d, d1] = go(
                remote(gath.at[0, d1], gath.at[4 - d, d1], p2_send.at[4 * n + d1], p2_recv.at[4 * n + d1], second(d))
            )

    forward(0)
    a_copy.wait_recv()
    b_copy.wait_recv()
    one_hots(lambda at, a: sib_tiles[at, pl.ds(a, 1), :], ROWS * NBINS)
    for i, block in enumerate((own_a, abuf)):
        for k in range(2):
            wa_ref[pl.ds(24 * i, 24), pl.ds(384 * k, 384)] = block[k].astype(F32)[:24]
    for n, d in enumerate(order):
        p1[n].wait_recv()
        forward(4 - d)

    x_acc[...] = jnp.zeros_like(x_acc)
    y_acc[...] = jnp.zeros_like(y_acc)

    def chunk(d2):
        weights = gath[d2].reshape(512, 384)

        def body(n, carry):
            rows = pl.ds(pl.multiple_of(512 * n, 512), 512)
            s = dot(hot[rows, pl.ds(512 * d2, 512)], weights)
            xs, ys = x_acc[...], y_acc[...]
            for a in range(8):
                w = wa_ref[pl.ds(8 * n + a, 1), :]
                piece = s[64 * a : 64 * a + 64]
                xs = xs + w[:, :384] * piece
                ys = ys + w[:, 384:] * piece
            x_acc[...] = xs
            y_acc[...] = ys
            return carry

        lax.fori_loop(0, 6, body, 0)

    chunk(0)
    for d in order:
        for d1 in range(4):
            p2[4 - d, d1].wait_recv()
        chunk(4 - d)

    xs = [x_acc[:, pl.ds(128 * t, 128)] for t in range(3)]
    ys = [y_acc[:, pl.ds(128 * t, 128)] for t in range(3)]
    signed = sign.astype(F32)
    sums = [xs[0] + xs[2], xs[1] + unpack(xs, 64), signed * (ys[0] - ys[2]), signed * (ys[1] - unpack(ys, 64))]
    for t in range(4):
        for k in range(8):
            part[k, :, pl.ds(128 * t, 128)] = sums[t][8 * k : 8 * k + 8]

    r1[place] = part[place]
    copies = []
    for d in range(1, 8):
        to = mod(place + d, 8)
        copies.append(go(remote(part.at[to], r1.at[place], r1_send.at[d - 1], r1_recv.at[d - 1], (chan, to))))
    for copy in copies:
        copy.wait_recv()

    def total(ref, n):
        value = ref[0]
        for i in range(1, n):
            value = value + ref[i]
        return value

    r2[quad] = total(r1, 8)
    copies = [
        go(remote(r2.at[quad], r2.at[quad], r2_send.at[d], r2_recv.at[d], pairs[d])) for d in range(3)
    ]
    for copy in copies:
        copy.wait_recv()
    r3[z] = total(r2, 4)
    copies = [
        go(remote(r3.at[z], r3.at[z], r3_send.at[d - 1], r3_recv.at[d - 1], (4 * mod(z + d, 8) + quad, place)))
        for d in range(1, 8)
    ]
    for load in loads[6:]:
        load.wait()
    for copy in copies:
        copy.wait_recv()
    hi, lo = halves(total(r3, 8))
    both = jnp.concatenate([hi.astype(F32), lo.astype(F32)], axis=0).astype(BF16)
    out = dot(both, lhi_ref[...]) + dot(both, llo_ref[...])
    out_ref[...] = out[:8] + out[8:]
    for copy in sends:
        copy.wait_send()


def solution(mesh):
    tables = make_tables()
    any_space = pl.BlockSpec(memory_space=pl.ANY)
    vmem = pl.BlockSpec(memory_space=pltpu.VMEM)
    dma = pltpu.SemaphoreType.DMA

    def step(traces, fir_taps, pair_bin):
        return pl.pallas_call(
            kernel,
            out_shape=jax.ShapeDtypeStruct((8, LAGS), F32),
            in_specs=[any_space, vmem, any_space] + [any_space] * len(tables),
            out_specs=vmem,
            scratch_shapes=[
                pltpu.VMEM((24, SAMPLES), F32),
                pltpu.VMEM((32, 256), F32),
                pltpu.VMEM((512, 256), BF16),
                pltpu.VMEM((512, 256), BF16),
                pltpu.VMEM((128, 512), F32),
                pltpu.VMEM((256, 256), BF16),
                pltpu.VMEM((512, 512), BF16),
                pltpu.VMEM((512, 512), BF16),
                pltpu.VMEM((5, 24, LEVEL), jnp.int32),
                pltpu.VMEM((384, 512), F32),
                pltpu.VMEM((5, 32, 384), BF16),
                pltpu.VMEM((2, 32, 384), BF16),
                pltpu.VMEM((2, 32, 384), BF16),
                pltpu.VMEM((2, 16, 24, 128), F32),
                pltpu.VMEM((16, 24, 128), F32),
                pltpu.VMEM((48, 768), F32),
                pltpu.VMEM((2 * ROWS * NBINS, 2048), BF16),
                pltpu.VMEM((4, 4, 128, 384), BF16),
                pltpu.VMEM((64, 384), F32),
                pltpu.VMEM((64, 384), F32),
                pltpu.VMEM((8, 8, 512), F32),
                pltpu.VMEM((8, 8, 512), F32),
                pltpu.VMEM((4, 8, 512), F32),
                pltpu.VMEM((8, 8, 512), F32),
                dma((8,)),
                dma((5,)),
                dma((4,)),
                dma((4,)),
                dma((2,)),
                dma((2,)),
                dma((3,)),
                dma((3,)),
                dma((12,)),
                dma((12,)),
                dma((7,)),
                dma((7,)),
                dma((3,)),
                dma((3,)),
                dma((7,)),
                dma((7,)),
            ],
            compiler_params=pltpu.CompilerParams(
                collective_id=0, has_side_effects=True, vmem_limit_bytes=56 * 2**20
            ),
            name="stack",
        )(traces, fir_taps.reshape(1, TAPS), pair_bin, *[jnp.asarray(t) for t in tables])

    return jax.shard_map(
        step,
        mesh=mesh,
        in_specs=(P(("chan", "bin"), None), P(), P(("chan", "bin"), None)),
        out_specs=P("bin", None),
        check_vma=False,
    )
```

time: 547 us -> 55.2 us (0.10)
  the two profiles are of different devices: /device:TPU:1 before, /device:TPU:24 now
where the time goes in v1:
time: 55.2 us; the launch traced here: 55 us
  Pallas kernels  53.7 us (97%)
  local copies, waits for them, and re-layouts  1.32 us (2%)
    pallas_call x1, Pallas kernels, step(): pl.pallas_call(kernel, out_shape=jax.ShapeDtypeStruct((8, LAGS), F32), in...  53.7 us
    unnamed x1, local copies, waits for them, and re-layouts  1.32 us

profile of v1, /device:TPU:24, one launch (start us, length us, event | category | flops | bytes accessed | tf_op | source)
XLA Modules:
  0.0 55.0 jit_solution(12393645746837876195)
XLA Ops:
  0.0 53.7 %stack.1 = f32[8,512]{1,0:T(8,128)} custom-call(f32[24,4096]{1,0:T(8,128)} %x_hbm.1, f32[1,64]{1,0:T(1,128)} %bitcast.1, s32[24,6144]{1,0:T(8,128)} %bins_hbm.1, f32[32,256]{1,0:T(8,128)} %constant.14.clone.tw_hbm, bf16[512,256]{1,0:T(8,128)(2,1)} %constant.15.clone.fhi_hbm, bf16[512,256]{1,0:T(8,128)(2,1)} %constant.16.clone.flo_hbm, ...), custom_call_target="tpu_custom_call" | custom-call | tf_op jit(solution)/shard_map/stack/pallas_call | solution.py:403
  53.7 1.3 %copy.12 = f32[8,512]{1,0:T(8,128)} copy(f32[8,512]{1,0:T(8,128)} %stack.1) | data formatting | bytes 32768

commit v2 on v1

v2 whole, which is shorter than its diff:
```python
import math

import jax
import jax.numpy as jnp
import numpy as np
from jax import lax
from jax.experimental import pallas as pl
from jax.experimental.pallas import tpu as pltpu
from jax.sharding import PartitionSpec as P

SAMPLES = 4096
TAPS = 64
BAND_LO = 64
NF = 192
MARGIN = 32
LAGS = 512
NBINS = 64
ROWS = 24
LEVEL = 768
MESH = pl.DeviceIdType.MESH
F32 = jnp.float32
BF16 = jnp.bfloat16


def lane_freqs():
    lane = np.arange(128)
    return np.concatenate([16 * (lane % 16) + 8 * j + lane // 16 for j in range(2)])


HALF = [(dx, dy, dc) for dc in (0, 1) for dx, dy in ((1, 2), (3, 1), (3, 3), (2, 3), (1, 0), (0, 1))]
HALF += [(dx, dy, dc) for dx, dy, dc in np.ndindex(3, 3, 2) if dx != 1 and dy != 1][::-1]
TIES = 12
DEPTH = 512


def geometry():
    table = np.zeros((8, DEPTH), np.int32)
    table[3], table[4] = -4096, 2
    for slot, h in enumerate(HALF):
        at = slice(ROWS * slot, ROWS * slot + ROWS)
        table[:3, at] = np.array(h)[:, None]
        table[3, at] = np.arange(ROWS)
        table[4, at] = slot >= TIES
    return table


def make_tables():
    e = lane_freqs()
    u = np.arange(256)
    ang = 2 * math.pi / SAMPLES * ((u[None, :] * np.arange(16)[:, None]) % SAMPLES)
    twiddle = np.concatenate([np.cos(ang), np.sin(ang)], 0).astype(np.float32)
    p = 2 + np.arange(128) % 16
    ang = 2 * math.pi / 256 * ((u[:, None] * p[None, :]) % 256)
    c, s = np.cos(ang), np.sin(ang)
    fine = np.concatenate([np.concatenate([c, -s], 1), np.concatenate([s, c], 1)], 0)
    ang = 2 * math.pi / SAMPLES * ((np.arange(128)[:, None] * (32 + e)[None, :]) % SAMPLES)
    taps = np.concatenate([np.cos(ang), -np.sin(ang)], 1)
    taps[TAPS:] = 0.0
    window = ((e[:, None] >= e[None, :] - MARGIN) & (e[:, None] < e[None, :] + MARGIN)) / (2.0 * MARGIN)
    f = e - MARGIN
    ok = (f >= 0) & (f < NF)
    phase = ((BAND_LO + np.where(ok, f, 0))[:, None] * (np.arange(LAGS) - LAGS // 2)[None, :]) % SAMPLES
    ang = 2 * math.pi / SAMPLES * phase
    lag = np.concatenate([np.cos(ang), -np.sin(ang)], 0) * (2.0 / SAMPLES) * np.concatenate([ok, ok])[:, None]
    return [t.astype(np.float32) for t in (twiddle, fine, taps, window, lag)] + [geometry()]


def dot(a, b, **kw):
    return jnp.dot(a, b, preferred_element_type=F32, **kw)


def halves(a):
    hi = a.astype(BF16)
    return hi, (a - hi.astype(F32)).astype(BF16)


def sixteen(x):
    root = math.sqrt(0.5)
    a = [x[k] + x[k + 8] for k in range(8)]
    b = [x[k] - x[k + 8] for k in range(8)]
    c = [a[k] + a[k + 4] for k in range(4)]
    d = [a[k] - a[k + 4] for k in range(4)]
    y = [None] * 9
    zero = jnp.zeros_like(x[0])
    even, odd = c[0] + c[2], c[1] + c[3]
    y[0] = (even + odd, zero)
    y[8] = (even - odd, zero)
    y[4] = (c[0] - c[2], c[3] - c[1])
    m, n = (d[1] - d[3]) * root, (d[1] + d[3]) * root
    y[2] = (d[0] + m, -(n + d[2]))
    y[6] = (d[0] - m, d[2] - n)
    for r in (1, 3, 5, 7):
        re, im = b[0], b[4] * (-1.0 if r % 4 == 1 else 1.0)
        for k in (1, 2, 3):
            re = re + (b[k] - b[8 - k]) * math.cos(math.pi * k * r / 8)
            im = im - (b[k] + b[8 - k]) * math.sin(math.pi * k * r / 8)
        y[r] = (re, im)
    return y


def whiten(x_ref, taps, tw_ref, fine_ref, tap_table, window, t_ref):
    def body(i, carry):
        rows = pl.ds(pl.multiple_of(8 * i, 8), 8)
        for j in range(2):
            lanes = pl.ds(128 * j, 128)
            y = sixteen([x_ref[rows, pl.ds(256 * w + 128 * j, 128)] for w in range(16)])
            for r in range(16):
                re, im = y[min(r, 16 - r)]
                if r > 8:
                    im = -im
                if r:
                    c, s = tw_ref[pl.ds(r, 1), lanes], tw_ref[pl.ds(16 + r, 1), lanes]
                    re, im = re * c + im * s, im * c - re * s
                at = pl.ds(pl.multiple_of(24 * r + 8 * i, 8), 8)
                t_ref[at, lanes] = re
                t_ref[at, pl.ds(256 + 128 * j, 128)] = im
        return carry

    lax.fori_loop(0, 3, body, 0)
    hi, lo = halves(t_ref[...])
    fine, fine_lo = halves(fine_ref[...])
    z = dot(hi, fine) + dot(lo, fine) + dot(hi, fine_lo)
    lane = lax.broadcasted_iota(jnp.int32, (24, 128), 1)
    ext = []
    for part in range(2):
        for j in range(2):
            tile = jnp.zeros((24, 128), F32)
            for r in range(8):
                piece = z[24 * (8 * j + r) : 24 * (8 * j + r) + 24, 128 * part : 128 * part + 128]
                tile = jnp.where(lane // 16 == r, piece, tile)
            ext.append(tile)
    padded = jnp.concatenate([taps, jnp.zeros((1, 64), F32)], axis=1)
    shifted = pltpu.roll(jnp.broadcast_to(padded, (128, 128)), 0, 1, stride=1, stride_axis=0)
    gains = dot(shifted, tap_table[...], precision=lax.Precision.HIGHEST)
    last = jnp.where(lane >= 64, x_ref[:, pl.ds(SAMPLES - 128, 128)], 0.0)
    cut = dot(last, gains, precision=lax.Precision.HIGHEST)
    h = [gains[0:1, 128 * k : 128 * k + 128] for k in range(4)]
    re = [h[j] * ext[j] - h[2 + j] * ext[2 + j] - cut[:, 128 * j : 128 * j + 128] for j in range(2)]
    im = [h[j] * ext[2 + j] + h[2 + j] * ext[j] - cut[:, 256 + 128 * j : 384 + 128 * j] for j in range(2)]
    power = jnp.concatenate([re[j] * re[j] + im[j] * im[j] for j in range(2)], axis=1)
    one = power.astype(BF16)
    rest = power - one.astype(F32)
    two = rest.astype(BF16)
    three = (rest - two.astype(F32)).astype(BF16)
    win = window[...].astype(BF16)
    smooth = dot(one, win) + dot(two, win) + dot(three, win)
    scale = 1.0 / jnp.sqrt(smooth + 1e-06)
    r0, r1 = (re[j] * scale[:, 128 * j : 128 * j + 128] for j in range(2))
    i0, i1 = (im[j] * scale[:, 128 * j : 128 * j + 128] for j in range(2))
    slot = lane % 16
    band = (slot >= 2) & (slot < 14)

    def pack(a, b, c, d):
        return [
            jnp.where(band, t, pltpu.roll(d, s, 1)) for t, s in ((a, 12), (b, 8), (c, 4))
        ]

    return pack(r0, r1, i0, i1)


def swap(tiles):
    a, b, c = tiles
    slot = lax.broadcasted_iota(jnp.int32, (ROWS, 128), 1) % 16
    band = (slot >= 2) & (slot < 14)
    full = (c, unpack(tiles, ROWS), a)
    return [jnp.where(band, t, pltpu.roll(b, s, 1)) for t, s in zip(full, (12, 8, 4))]


def unpack(tiles, rows):
    slot = lax.broadcasted_iota(jnp.int32, (rows, 128), 1) % 16
    a, b, c = (pltpu.roll(t, s, 1) for t, s in zip(tiles, (116, 120, 124)))
    return jnp.where(slot < 6, a, jnp.where(slot < 10, b, c))


def mod(a, n):
    return lax.rem(a, jnp.int32(n))


def fold(rows, width):
    parts = [rows[16:, i : i + width] for i in range(0, rows.shape[1], width)]
    if parts[1].shape[1] < width:
        parts[1] = jnp.concatenate([parts[1], jnp.zeros((8, width - parts[1].shape[1]), F32)], axis=1)
    return jnp.concatenate([rows[:16], jnp.concatenate(parts, axis=0)], axis=1).astype(BF16)


def unfold(block, cols, width):
    wide = block.astype(F32)
    tail = [wide[:8, cols:], wide[8:, cols : 2 * cols - width]]
    return jnp.concatenate([wide[:, :cols], jnp.concatenate(tail, axis=1)], axis=0)


def kernel(
    x_hbm, taps_ref, bins_hbm, tw_hbm, fine_hbm, tap_hbm, win_hbm, lag_hbm, geo_hbm,
    out_ref,
    x_ref, tw_ref, fine_ref, tap_ref, win_ref, lag_ref, geo_ref, lev_ref, t_ref, lhi_ref, llo_ref,
    mine, bbuf, abuf, bsend, brecv, codes_ref, wa_ref, hot0, hot1, bmat, s0, s1, x_acc, y_acc, part, r1, r2, r3,
    in_sem, lev_sem, b_send, b_recv, a_send, a_recv, c_send, c_recv,
    r1_send, r1_recv, r2_send, r2_recv, r3_send, r3_recv,
):
    chan, place = lax.axis_index("chan"), lax.axis_index("bin")
    z, quad = lax.div(chan, jnp.int32(4)), mod(chan, 4)
    y_lo, core = lax.div(quad, jnp.int32(2)), mod(quad, 2)
    y_hi, x = lax.div(place, jnp.int32(4)), mod(place, 4)
    y = 2 * y_hi + y_lo
    me = 16 * y_lo + 8 * core + place

    def device(dx, dy, dz, dc):
        xx, yy, zz, cc = mod(x + dx, 4), mod(y + dy, 4), mod(z + dz, 8), mod(core + dc, 2)
        return (4 * zz + 2 * mod(yy, 2) + cc, 4 * lax.div(yy, jnp.int32(2)) + xx)

    lev_loads = [
        pltpu.make_async_copy(
            bins_hbm.at[:, pl.ds(pl.multiple_of(mod(z + d, 8) * LEVEL, 128), LEVEL)], lev_ref.at[d], lev_sem.at[d]
        )
        for d in range(8)
    ]
    loads = [
        pltpu.make_async_copy(src, dst, in_sem.at[i])
        for i, (src, dst) in enumerate(
            (
                (x_hbm, x_ref), (tw_hbm, tw_ref), (fine_hbm, fine_ref), (tap_hbm, tap_ref), (win_hbm, win_ref),
                (geo_hbm, geo_ref), (lag_hbm, lag_ref),
            )
        )
    ]
    for load in loads[:5] + lev_loads + loads[5:]:
        load.start()

    plane = [h for h in np.ndindex(4, 4, 2) if any(h)]
    plane.sort(key=lambda h: -(min(h[0], 4 - h[0]) + min(h[1], 4 - h[1])))
    plane = [tuple(map(int, h)) for h in plane]
    friends = [device(dx, dy, 0, dc) for dx, dy, dc in plane] + [device(0, 0, d, 0) for d in (4, 3, 5, 2, 6, 1, 7)]
    barrier = pltpu.get_barrier_semaphore()
    for friend in friends:
        pl.semaphore_signal(barrier, inc=1, device_id=friend, device_id_type=MESH)

    def remote(src, dst, send, recv, to):
        return pltpu.make_async_remote_copy(
            src_ref=src, dst_ref=dst, send_sem=send, recv_sem=recv, device_id=to, device_id_type=MESH
        )

    sibling = device(0, 0, 0, 1)
    for load in loads[:5]:
        load.wait()
    white = whiten(x_ref, taps_ref[...], tw_ref, fine_ref, tap_ref, win_ref, t_ref)
    mine[...] = fold(jnp.concatenate(white, axis=1), 256)
    pl.semaphore_wait(barrier, len(friends))

    far_first = sorted(range(len(HALF) - 1), key=lambda n: -sum(min(v, 4 - v) for v in HALF[n][:2]))
    for n in far_first:
        h = HALF[n]
        remote(mine, bbuf.at[n], b_send, b_recv, device(4 - h[0], 4 - h[1], 0, h[2])).start()
    order = (1, 7, 2, 6, 3, 5, 4)
    slot_of = {d: n for n, d in enumerate(order)}
    for d in order:
        n = slot_of[8 - d]
        remote(mine, abuf.at[n], a_send, a_recv.at[n], device(0, 0, d, 0)).start()

    loads[5].wait()
    dx, dy, dc = (geo_ref[pl.ds(i, 1), :] for i in range(3))
    kind = geo_ref[pl.ds(4, 1), :]
    xx, yy, cc = (x + dx) & 3, (y + dy) & 3, (core + dc) & 1
    source = 24 * (16 * (yy & 1) + 8 * cc + 4 * (yy >> 1) + xx) + geo_ref[pl.ds(3, 1), :]
    pick = (lax.broadcasted_iota(jnp.int32, (LEVEL, DEPTH), 0) == source).astype(F32).astype(BF16)
    for load in lev_loads:
        load.wait()
    picked = dot(lev_ref[...].reshape(8 * ROWS, LEVEL).astype(F32).astype(BF16), pick)
    for d in order:
        above = (mod(z + d, 8) > z).astype(jnp.int32)
        keep = jnp.broadcast_to(kind <= above, (ROWS, DEPTH))
        bsend[d - 1] = fold(jnp.where(keep, picked[ROWS * d : ROWS * d + ROWS], -1.0), 256)
    for d in order:
        n = slot_of[8 - d]
        remote(bsend.at[d - 1], brecv.at[n], c_send, c_recv.at[n], device(0, 0, d, 0)).start()
    own = 24 * me + lax.broadcasted_iota(jnp.int32, (ROWS, DEPTH), 0)
    codes_ref[pl.ds(0, ROWS), :] = jnp.where((kind < 2) & (source > own), picked[:ROWS], -1.0)
    codes_ref[pl.ds(ROWS, ROWS), :] = jnp.where((kind < 1) & (source < own), picked[:ROWS], -1.0)

    def set_rows(slot, rows, sign):
        tiles = [rows[:, 128 * t : 128 * t + 128] for t in range(3)]
        at = pl.ds(pl.multiple_of(ROWS * slot, 8), ROWS)
        for t, (one, two) in enumerate(zip(tiles, swap(tiles))):
            wa_ref[at, pl.ds(128 * t, 128)] = one
            wa_ref[at, pl.ds(384 + 128 * t, 128)] = two * sign

    def block_of(ref):
        return unfold(ref[...], 384, 256)

    bins = lax.broadcasted_iota(jnp.int32, (64, 128), 0).astype(F32).astype(BF16)

    def one_hots(out, slot, part):
        codes = codes_ref[pl.ds(pl.multiple_of(ROWS * slot, 8), ROWS), :]
        for a in range(12):
            row = codes[12 * part + a : 12 * part + a + 1]
            for t in range(4):
                lanes = pl.ds(128 * t, 128)
                code = jnp.broadcast_to(row[:, 128 * t : 128 * t + 128], (16, 128)).astype(BF16)
                for k in range(4):
                    out[pl.ds(64 * a + 16 * k, 16), lanes] = jnp.where(
                        code == bins[16 * k : 16 * k + 16], jnp.ones((), BF16), jnp.zeros((), BF16)
                    )

    def take(slot, part, ref):
        rows = pl.ds(pl.multiple_of(ROWS * slot, 8), ROWS)
        for t in range(3):
            lanes, more = pl.ds(128 * t, 128), pl.ds(384 + 128 * t, 128)
            w, v = wa_ref[rows, lanes], wa_ref[rows, more]
            xs, ys = x_acc[:, lanes], y_acc[:, lanes]
            for a in range(12):
                at = 12 * part + a
                piece = ref[pl.ds(64 * a, 64), lanes]
                xs = xs + w[at : at + 1] * piece
                ys = ys + v[at : at + 1] * piece
            x_acc[:, lanes] = xs
            y_acc[:, lanes] = ys

    one_hots(hot0, 0, 0)
    rows = block_of(mine)
    set_rows(0, rows, 1.0)
    set_rows(1, rows, -1.0)
    x_acc[...] = jnp.zeros_like(x_acc)
    y_acc[...] = jnp.zeros_like(y_acc)
    s1[...] = jnp.zeros_like(s1)
    loads[6].wait()
    lag_hi, lag_lo = halves(lag_ref[...])
    lhi_ref[...] = lag_hi
    llo_ref[...] = lag_lo
    blocks = len(HALF)
    bmat[pl.ds(ROWS * blocks, DEPTH - ROWS * blocks), :] = jnp.zeros((DEPTH - ROWS * blocks, 384), BF16)
    remote(bbuf, bbuf, b_send, b_recv, sibling).wait_recv()
    for n in range(0, blocks, 2):
        two = [block_of(bbuf.at[m]) if m < blocks - 1 else rows for m in (n, n + 1)]
        bmat[pl.ds(ROWS * n, 2 * ROWS), :] = jnp.concatenate(two, axis=0).astype(BF16)

    def body(slot, carry):
        after = slot + 1

        @pl.when((slot > 0) & (slot < 8))
        def _():
            n = slot - 1
            remote(brecv.at[n], brecv.at[n], c_send, c_recv.at[n], sibling).wait_recv()
            remote(abuf.at[n], abuf.at[n], a_send, a_recv.at[n], sibling).wait_recv()
            codes_ref[pl.ds(pl.multiple_of(ROWS * after, 8), ROWS), :] = unfold(brecv[n], 512, 256)
            k = lax.div(after, jnp.int32(2))
            d = k + mod(after, 2) * (8 - 2 * k)
            below = (mod(z + d, 8) < z).astype(F32)
            set_rows(after, block_of(abuf.at[n]), 2.0 * below - 1.0)

        s0[...] = dot(hot0[...], bmat[...])
        one_hots(hot1, slot, 1)
        take(jnp.maximum(slot - 1, 0), 1, s1)
        s1[...] = dot(hot1[...], bmat[...])
        one_hots(hot0, jnp.minimum(after, 8), 0)
        take(slot, 0, s0)
        return carry

    lax.fori_loop(0, 9, body, 0)
    take(8, 1, s1)

    xs = [x_acc[:, pl.ds(128 * t, 128)] for t in range(3)]
    ys = [y_acc[:, pl.ds(128 * t, 128)] for t in range(3)]
    sums = [xs[0] + xs[2], xs[1] + unpack(xs, 64), ys[0] - ys[2], ys[1] - unpack(ys, 64)]
    for t in range(4):
        for k in range(8):
            part[k, t] = sums[t][8 * k : 8 * k + 8]

    at = 4 * place + quad
    r1[at] = part[place, quad]
    for n, (dx, dy, dc) in enumerate(plane):
        to = device(dx, dy, 0, dc)
        remote(part.at[to[1], mod(to[0], 4)], r1.at[at], r1_send, r1_recv, to).start()
    remote(r1.at[pl.ds(0, 31)], r1.at[pl.ds(0, 31)], r1_send, r1_recv, sibling).wait_recv()

    def total(ref, n):
        values = [ref[i] for i in range(n)]
        while len(values) > 1:
            values = [a + b for a, b in zip(values[::2], values[1::2])]
        return values[0]

    r2[z] = total(r1, 32)
    for d in (4, 3, 5, 2, 6, 1, 7):
        remote(r2.at[z], r2.at[z], r2_send, r2_recv, device(0, 0, d, 0)).start()
    remote(r2.at[pl.ds(0, 7)], r2.at[pl.ds(0, 7)], r2_send, r2_recv, sibling).wait_recv()
    r3[quad] = total(r2, 8)
    for d in range(1, 4):
        to = (4 * z + mod(quad + d, 4), place)
        remote(r3.at[quad], r3.at[quad], r3_send, r3_recv, to).start()
    remote(r3.at[pl.ds(0, 3)], r3.at[pl.ds(0, 3)], r3_send, r3_recv, sibling).wait_recv()
    hi, lo = halves(jnp.concatenate([r3[t] for t in range(4)], axis=1))
    both = jnp.concatenate([hi.astype(F32), lo.astype(F32)], axis=0).astype(BF16)
    out = dot(both, lhi_ref[...]) + dot(both, llo_ref[...])
    out_ref[...] = out[:8] + out[8:]
    for src, send, recv in (
        (bbuf, b_send, b_recv), (abuf, a_send, a_recv.at[0]), (bsend, c_send, c_recv.at[0]),
        (r1.at[pl.ds(0, 31)], r1_send, r1_recv), (r2.at[pl.ds(0, 7)], r2_send, r2_recv), (r3.at[pl.ds(0, 3)], r3_send, r3_recv),
    ):
        remote(src, src, send, recv, sibling).wait_send()


def solution(mesh):
    tables = make_tables()
    any_space = pl.BlockSpec(memory_space=pl.ANY)
    vmem = pl.BlockSpec(memory_space=pltpu.VMEM)
    dma = pltpu.SemaphoreType.DMA
    n = len(HALF)

    def step(traces, fir_taps, pair_bin):
        return pl.pallas_call(
            kernel,
            out_shape=jax.ShapeDtypeStruct((8, LAGS), F32),
            in_specs=[any_space, vmem, any_space] + [any_space] * len(tables),
            out_specs=vmem,
            scratch_shapes=[
                pltpu.VMEM((ROWS, SAMPLES), F32),
                *[pltpu.VMEM(t.shape, t.dtype) for t in tables],
                pltpu.VMEM((8, ROWS, LEVEL), jnp.int32),
                pltpu.VMEM((16 * ROWS, 512), F32),
                pltpu.VMEM((512, 512), BF16),
                pltpu.VMEM((512, 512), BF16),
                pltpu.VMEM((16, 640), BF16),
                pltpu.VMEM((n - 1, 16, 640), BF16),
                pltpu.VMEM((7, 16, 640), BF16),
                pltpu.VMEM((7, 16, 768), BF16),
                pltpu.VMEM((7, 16, 768), BF16),
                pltpu.VMEM((9 * ROWS, DEPTH), F32),
                pltpu.VMEM((9 * ROWS, 768), F32),
                pltpu.VMEM((12 * NBINS, DEPTH), BF16),
                pltpu.VMEM((12 * NBINS, DEPTH), BF16),
                pltpu.VMEM((DEPTH, 384), BF16),
                pltpu.VMEM((12 * NBINS, 384), F32),
                pltpu.VMEM((12 * NBINS, 384), F32),
                pltpu.VMEM((64, 384), F32),
                pltpu.VMEM((64, 384), F32),
                pltpu.VMEM((8, 4, 8, 128), F32),
                pltpu.VMEM((32, 8, 128), F32),
                pltpu.VMEM((8, 8, 128), F32),
                pltpu.VMEM((4, 8, 128), F32),
                dma((7,)),
                dma((8,)),
                dma(()),
                dma(()),
                dma(()),
                dma((7,)),
                dma(()),
                dma((7,)),
                dma(()),
                dma(()),
                dma(()),
                dma(()),
                dma(()),
                dma(()),
            ],
            compiler_params=pltpu.CompilerParams(
                collective_id=0, has_side_effects=True, vmem_limit_bytes=56 * 2**20
            ),
            name="stack",
        )(traces, fir_taps.reshape(1, TAPS), pair_bin, *[jnp.asarray(t) for t in tables])

    return jax.shard_map(
        step,
        mesh=mesh,
        in_specs=(P(("chan", "bin"), None), P(), P(("chan", "bin"), None)),
        out_specs=P("bin", None),
        check_vma=False,
    )
```

time: 55.2 us -> 43.7 us (0.79)
  the two profiles are of different devices: /device:TPU:24 before, /device:TPU:1 now
where the time goes in v2:
time: 43.7 us; the launch traced here: 43.5 us
  Pallas kernels  42.2 us (97%)
  local copies, waits for them, and re-layouts  1.32 us (3%)
    pallas_call x1, Pallas kernels, step(): pl.pallas_call(kernel, out_shape=jax.ShapeDtypeStruct((8, LAGS), F32), in...  42.2 us
    unnamed x1, local copies, waits for them, and re-layouts  1.32 us

profile of v2, /device:TPU:1, one launch (start us, length us, event | category | flops | bytes accessed | tf_op | source)
XLA Modules:
  0.0 43.5 jit_solution(7526989510505590273)
XLA Ops:
  0.0 42.2 %stack.1 = f32[8,512]{1,0:T(8,128)} custom-call(f32[24,4096]{1,0:T(8,128)} %x_hbm.1, f32[1,64]{1,0:T(1,128)} %bitcast.1, s32[24,6144]{1,0:T(8,128)} %bins_hbm.1, f32[32,256]{1,0:T(8,128)} %constant.12.clone.tw_hbm, f32[512,256]{1,0:T(8,128)} %constant.13.clone.fine_hbm, f32[128,512]{1,0:T(8,128)} %constant.14.clone.tap_hbm, ...), custom_call_target="tpu_custom_call" | custom-call | tf_op jit(solution)/shard_map/stack/pallas_call | solution.py:408
  42.2 1.3 %copy.11 = f32[8,512]{1,0:T(8,128)} copy(f32[8,512]{1,0:T(8,128)} %stack.1) | data formatting | bytes 32768

commit v3 on v2

--- a/solution.py
+++ b/solution.py
@@ -27,20 +27,20 @@
     return np.concatenate([16 * (lane % 16) + 8 * j + lane // 16 for j in range(2)])
 
 
-HALF = [(dx, dy, dc) for dc in (0, 1) for dx, dy in ((1, 2), (3, 1), (3, 3), (2, 3), (1, 0), (0, 1))]
-HALF += [(dx, dy, dc) for dx, dy, dc in np.ndindex(3, 3, 2) if dx != 1 and dy != 1][::-1]
-TIES = 12
+HALF = [(2, 2), (1, 2), (2, 3), (3, 1), (3, 3), (2, 0), (0, 2), (1, 0), (0, 1), (0, 0)]
+FAR = 3
 DEPTH = 512
 
 
 def geometry():
     table = np.zeros((8, DEPTH), np.int32)
     table[3], table[4] = -4096, 2
-    for slot, h in enumerate(HALF):
+    for slot in range(2 * len(HALF)):
         at = slice(ROWS * slot, ROWS * slot + ROWS)
-        table[:3, at] = np.array(h)[:, None]
+        dc, n = divmod(slot, len(HALF))
+        table[:3, at] = np.array((*HALF[n], dc))[:, None]
         table[3, at] = np.arange(ROWS)
-        table[4, at] = slot >= TIES
+        table[4, at] = not any(v % 2 for v in HALF[n])
     return table
 
 
@@ -52,17 +52,15 @@
     p = 2 + np.arange(128) % 16
     ang = 2 * math.pi / 256 * ((u[:, None] * p[None, :]) % 256)
     c, s = np.cos(ang), np.sin(ang)
-    fine = np.concatenate([np.concatenate([c, -s], 1), np.concatenate([s, c], 1)], 0)
-    ang = 2 * math.pi / SAMPLES * ((np.arange(128)[:, None] * (32 + e)[None, :]) % SAMPLES)
+    fine = np.concatenate([c, s], 1)
+    ang = 2 * math.pi / SAMPLES * ((np.arange(TAPS)[:, None] * (32 + e)[None, :]) % SAMPLES)
     taps = np.concatenate([np.cos(ang), -np.sin(ang)], 1)
-    taps[TAPS:] = 0.0
-    window = ((e[:, None] >= e[None, :] - MARGIN) & (e[:, None] < e[None, :] + MARGIN)) / (2.0 * MARGIN)
     f = e - MARGIN
     ok = (f >= 0) & (f < NF)
     phase = ((BAND_LO + np.where(ok, f, 0))[:, None] * (np.arange(LAGS) - LAGS // 2)[None, :]) % SAMPLES
     ang = 2 * math.pi / SAMPLES * phase
     lag = np.concatenate([np.cos(ang), -np.sin(ang)], 0) * (2.0 / SAMPLES) * np.concatenate([ok, ok])[:, None]
-    return [t.astype(np.float32) for t in (twiddle, fine, taps, window, lag)] + [geometry()]
+    return [t.astype(np.float32) for t in (twiddle, fine, taps, lag)] + [geometry()]
 
 
 def dot(a, b, **kw):
@@ -98,12 +96,28 @@
     return y
 
 
-def whiten(x_ref, taps, tw_ref, fine_ref, tap_table, window, t_ref):
+def freq_of(shape, axis):
+    i = lax.broadcasted_iota(jnp.int32, shape, axis)
+    return 16 * (i & 15) + 8 * (i >> 7) + ((i >> 4) & 7)
+
+
+def whiten(x_ref, taps, tw_ref, fine_ref, tap_table, hi_ref, lo_ref, loads):
+    padded = jnp.concatenate([taps, jnp.zeros((1, 64), F32)], axis=1)
+    shifted = pltpu.roll(jnp.broadcast_to(padded, (128, 128)), 0, 1, stride=1, stride_axis=0)
+    target = freq_of((256, 256), 1)
+    apart = freq_of((256, 256), 0) - target
+    win = jnp.where((apart >= -MARGIN) & (apart < MARGIN), 0.5 / MARGIN, 0.0).astype(BF16)
+    loads["taps"].wait()
+    gains = dot(shifted[:, :TAPS], tap_table[...], precision=lax.Precision.HIGHEST)
+    loads["x"].wait()
+    loads["tw"].wait()
+
     def body(i, carry):
         rows = pl.ds(pl.multiple_of(8 * i, 8), 8)
         for j in range(2):
             lanes = pl.ds(128 * j, 128)
             y = sixteen([x_ref[rows, pl.ds(256 * w + 128 * j, 128)] for w in range(16)])
+            parts = []
             for r in range(16):
                 re, im = y[min(r, 16 - r)]
                 if r > 8:
@@ -111,27 +125,32 @@
                 if r:
                     c, s = tw_ref[pl.ds(r, 1), lanes], tw_ref[pl.ds(16 + r, 1), lanes]
                     re, im = re * c + im * s, im * c - re * s
-                at = pl.ds(pl.multiple_of(24 * r + 8 * i, 8), 8)
-                t_ref[at, lanes] = re
-                t_ref[at, pl.ds(256 + 128 * j, 128)] = im
+                parts.append((re, im))
+            for r in range(0, 16, 2):
+                at = pl.ds(pl.multiple_of(128 * i + 8 * r, 16), 16)
+                for k in range(2):
+                    hi, lo = halves(jnp.concatenate([parts[r][k], parts[r + 1][k]], axis=0))
+                    hi_ref[at, pl.ds(256 * k + 128 * j, 128)] = hi
+                    lo_ref[at, pl.ds(256 * k + 128 * j, 128)] = lo
         return carry
 
     lax.fori_loop(0, 3, body, 0)
-    hi, lo = halves(t_ref[...])
-    fine, fine_lo = halves(fine_ref[...])
-    z = dot(hi, fine) + dot(lo, fine) + dot(hi, fine_lo)
+    loads["fine"].wait()
+    both = fine_ref[...]
+    c, s = halves(both[:, :128]), halves(both[:, 128:])
+    fine = [jnp.concatenate([jnp.concatenate([c[k], -s[k]], 1), jnp.concatenate([s[k], c[k]], 1)], 0) for k in range(2)]
+    left = jnp.concatenate([hi_ref[...], lo_ref[...], hi_ref[...]], axis=1)
+    z = dot(left, jnp.concatenate([fine[0], fine[0], fine[1]], axis=0))
     lane = lax.broadcasted_iota(jnp.int32, (24, 128), 1)
     ext = []
     for part in range(2):
         for j in range(2):
             tile = jnp.zeros((24, 128), F32)
             for r in range(8):
-                piece = z[24 * (8 * j + r) : 24 * (8 * j + r) + 24, 128 * part : 128 * part + 128]
+                at = 8 * (8 * j + r)
+                piece = jnp.concatenate([z[128 * i + at : 128 * i + at + 8, 128 * part : 128 * part + 128] for i in range(3)], 0)
                 tile = jnp.where(lane // 16 == r, piece, tile)
             ext.append(tile)
-    padded = jnp.concatenate([taps, jnp.zeros((1, 64), F32)], axis=1)
-    shifted = pltpu.roll(jnp.broadcast_to(padded, (128, 128)), 0, 1, stride=1, stride_axis=0)
-    gains = dot(shifted, tap_table[...], precision=lax.Precision.HIGHEST)
     last = jnp.where(lane >= 64, x_ref[:, pl.ds(SAMPLES - 128, 128)], 0.0)
     cut = dot(last, gains, precision=lax.Precision.HIGHEST)
     h = [gains[0:1, 128 * k : 128 * k + 128] for k in range(4)]
@@ -142,7 +161,6 @@
     rest = power - one.astype(F32)
     two = rest.astype(BF16)
     three = (rest - two.astype(F32)).astype(BF16)
-    win = window[...].astype(BF16)
     smooth = dot(one, win) + dot(two, win) + dot(three, win)
     scale = 1.0 / jnp.sqrt(smooth + 1e-06)
     r0, r1 = (re[j] * scale[:, 128 * j : 128 * j + 128] for j in range(2))
@@ -190,11 +208,11 @@
 
 
 def kernel(
-    x_hbm, taps_ref, bins_hbm, tw_hbm, fine_hbm, tap_hbm, win_hbm, lag_hbm, geo_hbm,
+    x_hbm, taps_ref, bins_hbm, tw_hbm, fine_hbm, tap_hbm, lag_hbm, geo_hbm,
     out_ref,
-    x_ref, tw_ref, fine_ref, tap_ref, win_ref, lag_ref, geo_ref, lev_ref, t_ref, lhi_ref, llo_ref,
-    mine, bbuf, abuf, bsend, brecv, codes_ref, wa_ref, hot0, hot1, bmat, s0, s1, x_acc, y_acc, part, r1, r2, r3,
-    in_sem, lev_sem, b_send, b_recv, a_send, a_recv, c_send, c_recv,
+    x_ref, tw_ref, fine_ref, tap_ref, lag_ref, geo_ref, lev_ref, pick_ref, hi_ref, lo_ref, lhi_ref, llo_ref,
+    bbuf, abuf, bsend, brecv, codes_ref, wa_ref, hot0, hot1, bmat, s0, s1, x_acc, y_acc, part, r1, r2, r3,
+    in_sem, lev_sem, b_send, b_recv, s_send, s_recv, a_send, a_recv, c_send, c_recv,
     r1_send, r1_recv, r2_send, r2_recv, r3_send, r3_recv,
 ):
     chan, place = lax.axis_index("chan"), lax.axis_index("bin")
@@ -214,22 +232,22 @@
         )
         for d in range(8)
     ]
-    loads = [
-        pltpu.make_async_copy(src, dst, in_sem.at[i])
-        for i, (src, dst) in enumerate(
-            (
-                (x_hbm, x_ref), (tw_hbm, tw_ref), (fine_hbm, fine_ref), (tap_hbm, tap_ref), (win_hbm, win_ref),
-                (geo_hbm, geo_ref), (lag_hbm, lag_ref),
-            )
-        )
-    ]
-    for load in loads[:5] + lev_loads + loads[5:]:
+    copies = dict(
+        taps=(tap_hbm, tap_ref), x=(x_hbm, x_ref), tw=(tw_hbm, tw_ref), fine=(fine_hbm, fine_ref),
+        geo=(geo_hbm, geo_ref), lag=(lag_hbm, lag_ref),
+    )
+    loads = {name: pltpu.make_async_copy(*refs, in_sem.at[i]) for i, (name, refs) in enumerate(copies.items())}
+    for name in ("geo", "taps", "x", "tw", "fine"):
+        loads[name].start()
+    for load in lev_loads:
         load.start()
-
+    loads["lag"].start()
+
+    other = 1 - 2 * y_lo
     plane = [h for h in np.ndindex(4, 4, 2) if any(h)]
     plane.sort(key=lambda h: -(min(h[0], 4 - h[0]) + min(h[1], 4 - h[1])))
     plane = [tuple(map(int, h)) for h in plane]
-    friends = [device(dx, dy, 0, dc) for dx, dy, dc in plane] + [device(0, 0, d, 0) for d in (4, 3, 5, 2, 6, 1, 7)]
+    friends = [device(dx, dy, 0, dc) for dx, dy, dc in plane] + [device(0, e, d, 0) for d in (4, 3, 5, 2, 6, 1, 7) for e in (other, 0)]
     barrier = pltpu.get_barrier_semaphore()
     for friend in friends:
         pl.semaphore_signal(barrier, inc=1, device_id=friend, device_id_type=MESH)
@@ -240,41 +258,36 @@
         )
 
     sibling = device(0, 0, 0, 1)
-    for load in loads[:5]:
-        load.wait()
-    white = whiten(x_ref, taps_ref[...], tw_ref, fine_ref, tap_ref, win_ref, t_ref)
-    mine[...] = fold(jnp.concatenate(white, axis=1), 256)
-    pl.semaphore_wait(barrier, len(friends))
-
-    far_first = sorted(range(len(HALF) - 1), key=lambda n: -sum(min(v, 4 - v) for v in HALF[n][:2]))
-    for n in far_first:
-        h = HALF[n]
-        remote(mine, bbuf.at[n], b_send, b_recv, device(4 - h[0], 4 - h[1], 0, h[2])).start()
-    order = (1, 7, 2, 6, 3, 5, 4)
-    slot_of = {d: n for n, d in enumerate(order)}
-    for d in order:
-        n = slot_of[8 - d]
-        remote(mine, abuf.at[n], a_send, a_recv.at[n], device(0, 0, d, 0)).start()
-
-    loads[5].wait()
+    loads["geo"].wait()
     dx, dy, dc = (geo_ref[pl.ds(i, 1), :] for i in range(3))
     kind = geo_ref[pl.ds(4, 1), :]
     xx, yy, cc = (x + dx) & 3, (y + dy) & 3, (core + dc) & 1
     source = 24 * (16 * (yy & 1) + 8 * cc + 4 * (yy >> 1) + xx) + geo_ref[pl.ds(3, 1), :]
-    pick = (lax.broadcasted_iota(jnp.int32, (LEVEL, DEPTH), 0) == source).astype(F32).astype(BF16)
+    pick_ref[...] = (lax.broadcasted_iota(jnp.int32, (LEVEL, DEPTH), 0) == source).astype(F32).astype(BF16)
+    white = whiten(x_ref, taps_ref[...], tw_ref, fine_ref, tap_ref, hi_ref, lo_ref, loads)
+    blocks = len(HALF)
+    mine = bbuf.at[0, blocks - 1]
+    mine[...] = fold(jnp.concatenate(white, axis=1), 256)
+
+    order = (1, 7, 2, 6, 3, 5, 4)
+    slot_of = {d: n for n, d in enumerate(order)}
     for load in lev_loads:
         load.wait()
-    picked = dot(lev_ref[...].reshape(8 * ROWS, LEVEL).astype(F32).astype(BF16), pick)
+    picked = dot(lev_ref[...].reshape(8 * ROWS, LEVEL).astype(F32).astype(BF16), pick_ref[...])
+    pl.semaphore_wait(barrier, len(friends))
+    for n, (dx, dy) in enumerate(HALF[:-1]):
+        remote(mine, bbuf.at[0, n], b_send, b_recv.at[int(n >= FAR)], device(4 - dx, 4 - dy, 0, 0)).start()
     for d in order:
         above = (mod(z + d, 8) > z).astype(jnp.int32)
         keep = jnp.broadcast_to(kind <= above, (ROWS, DEPTH))
         bsend[d - 1] = fold(jnp.where(keep, picked[ROWS * d : ROWS * d + ROWS], -1.0), 256)
+    own = 24 * me + lax.broadcasted_iota(jnp.int32, (ROWS, DEPTH), 0)
+    codes_ref[pl.ds(0, ROWS), :] = jnp.where((kind < 2) & (source > own), picked[:ROWS], -1.0)
+    codes_ref[pl.ds(ROWS, ROWS), :] = jnp.where((kind < 1) & (source < own), picked[:ROWS], -1.0)
     for d in order:
         n = slot_of[8 - d]
         remote(bsend.at[d - 1], brecv.at[n], c_send, c_recv.at[n], device(0, 0, d, 0)).start()
-    own = 24 * me + lax.broadcasted_iota(jnp.int32, (ROWS, DEPTH), 0)
-    codes_ref[pl.ds(0, ROWS), :] = jnp.where((kind < 2) & (source > own), picked[:ROWS], -1.0)
-    codes_ref[pl.ds(ROWS, ROWS), :] = jnp.where((kind < 1) & (source < own), picked[:ROWS], -1.0)
+        remote(mine, abuf.at[n], a_send, a_recv.at[n], device(0, 0, d, 0)).start()
 
     def set_rows(slot, rows, sign):
         tiles = [rows[:, 128 * t : 128 * t + 128] for t in range(3)]
@@ -321,16 +334,34 @@
     x_acc[...] = jnp.zeros_like(x_acc)
     y_acc[...] = jnp.zeros_like(y_acc)
     s1[...] = jnp.zeros_like(s1)
-    loads[6].wait()
+    loads["lag"].wait()
     lag_hi, lag_lo = halves(lag_ref[...])
     lhi_ref[...] = lag_hi
     llo_ref[...] = lag_lo
-    blocks = len(HALF)
-    bmat[pl.ds(ROWS * blocks, DEPTH - ROWS * blocks), :] = jnp.zeros((DEPTH - ROWS * blocks, 384), BF16)
-    remote(bbuf, bbuf, b_send, b_recv, sibling).wait_recv()
-    for n in range(0, blocks, 2):
-        two = [block_of(bbuf.at[m]) if m < blocks - 1 else rows for m in (n, n + 1)]
-        bmat[pl.ds(ROWS * n, 2 * ROWS), :] = jnp.concatenate(two, axis=0).astype(BF16)
+    bmat[pl.ds(2 * ROWS * blocks, DEPTH - 2 * ROWS * blocks), :] = jnp.zeros((DEPTH - 2 * ROWS * blocks, 384), BF16)
+    groups = (pl.ds(FAR, blocks - FAR), pl.ds(0, FAR))
+    near = bbuf.at[0, pl.ds(FAR, blocks - 1 - FAR)]
+    far = bbuf.at[0, pl.ds(0, FAR)]
+
+    def share(k):
+        at = groups[k]
+        return remote(bbuf.at[0, at], bbuf.at[1, at], s_send, s_recv.at[k], sibling)
+
+    def assemble(k, first, last):
+        for n in range(first, last, 2):
+            two = [block_of(bbuf.at[k, m]) for m in (n, n + 1)]
+            bmat[pl.ds(ROWS * (blocks * k + n), 2 * ROWS), :] = jnp.concatenate(two, axis=0).astype(BF16)
+
+    remote(near, near, b_send, b_recv.at[1], sibling).wait_recv()
+    share(0).start()
+    assemble(0, FAR + 1, blocks)
+    remote(far, far, b_send, b_recv.at[0], sibling).wait_recv()
+    share(1).start()
+    assemble(0, 0, FAR + 1)
+    share(0).wait_recv()
+    assemble(1, FAR + 1, blocks)
+    share(1).wait_recv()
+    assemble(1, 0, FAR + 1)
 
     def body(slot, carry):
         after = slot + 1
@@ -339,12 +370,16 @@
         def _():
             n = slot - 1
             remote(brecv.at[n], brecv.at[n], c_send, c_recv.at[n], sibling).wait_recv()
+            codes_ref[pl.ds(pl.multiple_of(ROWS * after, 8), ROWS), :] = unfold(brecv[n], 512, 256)
+
+        @pl.when(slot > 1)
+        def _():
+            n = slot - 2
             remote(abuf.at[n], abuf.at[n], a_send, a_recv.at[n], sibling).wait_recv()
-            codes_ref[pl.ds(pl.multiple_of(ROWS * after, 8), ROWS), :] = unfold(brecv[n], 512, 256)
-            k = lax.div(after, jnp.int32(2))
-            d = k + mod(after, 2) * (8 - 2 * k)
+            k = lax.div(slot, jnp.int32(2))
+            d = k + mod(slot, 2) * (8 - 2 * k)
             below = (mod(z + d, 8) < z).astype(F32)
-            set_rows(after, block_of(abuf.at[n]), 2.0 * below - 1.0)
+            set_rows(slot, block_of(abuf.at[n]), 2.0 * below - 1.0)
 
         s0[...] = dot(hot0[...], bmat[...])
         one_hots(hot1, slot, 1)
@@ -377,22 +412,23 @@
             values = [a + b for a, b in zip(values[::2], values[1::2])]
         return values[0]
 
-    r2[z] = total(r1, 32)
-    for d in (4, 3, 5, 2, 6, 1, 7):
-        remote(r2.at[z], r2.at[z], r2_send, r2_recv, device(0, 0, d, 0)).start()
-    remote(r2.at[pl.ds(0, 7)], r2.at[pl.ds(0, 7)], r2_send, r2_recv, sibling).wait_recv()
-    r3[quad] = total(r2, 8)
-    for d in range(1, 4):
-        to = (4 * z + mod(quad + d, 4), place)
-        remote(r3.at[quad], r3.at[quad], r3_send, r3_recv, to).start()
-    remote(r3.at[pl.ds(0, 3)], r3.at[pl.ds(0, 3)], r3_send, r3_recv, sibling).wait_recv()
-    hi, lo = halves(jnp.concatenate([r3[t] for t in range(4)], axis=1))
+    r2[y_lo, z] = total(r1, 32)
+    for d in (4, 3, 5, 2, 6, 1, 7, 0):
+        for e in (other, 0) if d else (other,):
+            remote(r2.at[y_lo, z], r2.at[y_lo, z], r2_send, r2_recv, device(0, e, d, 0)).start()
+    most = r1.at[pl.ds(0, 15)]
+    remote(most, most, r2_send, r2_recv, sibling).wait_recv()
+    for k in range(2):
+        r3[core, k] = total(r2.at[k], 8)
+    remote(r3.at[core], r3.at[core], r3_send, r3_recv, sibling).start()
+    remote(r3.at[core], r3.at[core], r3_send, r3_recv, sibling).wait_recv()
+    hi, lo = halves(jnp.concatenate([r3[t % 2, t // 2] for t in range(4)], axis=1))
     both = jnp.concatenate([hi.astype(F32), lo.astype(F32)], axis=0).astype(BF16)
     out = dot(both, lhi_ref[...]) + dot(both, llo_ref[...])
     out_ref[...] = out[:8] + out[8:]
     for src, send, recv in (
-        (bbuf, b_send, b_recv), (abuf, a_send, a_recv.at[0]), (bsend, c_send, c_recv.at[0]),
-        (r1.at[pl.ds(0, 31)], r1_send, r1_recv), (r2.at[pl.ds(0, 7)], r2_send, r2_recv), (r3.at[pl.ds(0, 3)], r3_send, r3_recv),
+        (bbuf.at[0, pl.ds(0, blocks - 1)], b_send, b_recv.at[0]), (bbuf.at[0], s_send, s_recv.at[0]), (abuf, a_send, a_recv.at[0]), (bsend, c_send, c_recv.at[0]),
+        (r1.at[pl.ds(0, 31)], r1_send, r1_recv), (most, r2_send, r2_recv), (r3.at[0], r3_send, r3_recv),
     ):
         remote(src, src, send, recv, sibling).wait_send()
 
@@ -402,7 +438,6 @@
     any_space = pl.BlockSpec(memory_space=pl.ANY)
     vmem = pl.BlockSpec(memory_space=pltpu.VMEM)
     dma = pltpu.SemaphoreType.DMA
-    n = len(HALF)
 
     def step(traces, fir_taps, pair_bin):
         return pl.pallas_call(
@@ -414,11 +449,12 @@
                 pltpu.VMEM((ROWS, SAMPLES), F32),
                 *[pltpu.VMEM(t.shape, t.dtype) for t in tables],
                 pltpu.VMEM((8, ROWS, LEVEL), jnp.int32),
-                pltpu.VMEM((16 * ROWS, 512), F32),
+                pltpu.VMEM((LEVEL, DEPTH), BF16),
+                pltpu.VMEM((16 * ROWS, 512), BF16),
+                pltpu.VMEM((16 * ROWS, 512), BF16),
                 pltpu.VMEM((512, 512), BF16),
                 pltpu.VMEM((512, 512), BF16),
-                pltpu.VMEM((16, 640), BF16),
-                pltpu.VMEM((n - 1, 16, 640), BF16),
+                pltpu.VMEM((2, len(HALF), 16, 640), BF16),
                 pltpu.VMEM((7, 16, 640), BF16),
                 pltpu.VMEM((7, 16, 768), BF16),
                 pltpu.VMEM((7, 16, 768), BF16),
@@ -433,12 +469,14 @@
                 pltpu.VMEM((64, 384), F32),
                 pltpu.VMEM((8, 4, 8, 128), F32),
                 pltpu.VMEM((32, 8, 128), F32),
-                pltpu.VMEM((8, 8, 128), F32),
-                pltpu.VMEM((4, 8, 128), F32),
+                pltpu.VMEM((2, 8, 8, 128), F32),
+                pltpu.VMEM((2, 2, 8, 128), F32),
                 dma((7,)),
                 dma((8,)),
                 dma(()),
-                dma(()),
+                dma((2,)),
+                dma(()),
+                dma((2,)),
                 dma(()),
                 dma((7,)),
                 dma(()),

time: 43.7 us -> 41.8 us (0.957)
  Pallas kernels: 42.2 us -> 40.3 us
    pallas_call x1, Pallas kernels: 42.2 us -> 40.3 us  [step(): pl.pallas_call(kernel, out_shape=jax.ShapeDtypeStruct((8, LAGS), F32), in...]
where the time goes in v3:
time: 41.8 us; the launch traced here: 41.6 us
  Pallas kernels  40.3 us (96%)
  local copies, waits for them, and re-layouts  1.32 us (3%)
    pallas_call x1, Pallas kernels, step(): pl.pallas_call(kernel, out_shape=jax.ShapeDtypeStruct((8, LAGS), F32), in...  40.3 us
    unnamed x1, local copies, waits for them, and re-layouts  1.32 us

profile of v3, /device:TPU:1, one launch (start us, length us, event | category | flops | bytes accessed | tf_op | source)
XLA Modules:
  0.0 41.6 jit_solution(9743563117629164739)
XLA Ops:
  0.0 40.3 %stack.1 = f32[8,512]{1,0:T(8,128)} custom-call(f32[24,4096]{1,0:T(8,128)} %x_hbm.1, f32[1,64]{1,0:T(1,128)} %bitcast.1, s32[24,6144]{1,0:T(8,128)} %bins_hbm.1, f32[32,256]{1,0:T(8,128)} %constant.10.clone.tw_hbm, f32[256,256]{1,0:T(8,128)} %constant.11.clone.fine_hbm, f32[64,512]{1,0:T(8,128)} %constant.12.clone.tap_hbm, ...), custom_call_target="tpu_custom_call" | custom-call | tf_op jit(solution)/shard_map/stack/pallas_call | solution.py:443
  40.3 1.3 %copy.10 = f32[8,512]{1,0:T(8,128)} copy(f32[8,512]{1,0:T(8,128)} %stack.1) | data formatting | bytes 32768

commit v4 on v3

--- a/solution.py
+++ b/solution.py
@@ -28,19 +28,20 @@
 
 
 HALF = [(2, 2), (1, 2), (2, 3), (3, 1), (3, 3), (2, 0), (0, 2), (1, 0), (0, 1), (0, 0)]
-FAR = 3
+FAR = 5
 DEPTH = 512
 
 
 def geometry():
     table = np.zeros((8, DEPTH), np.int32)
     table[3], table[4] = -4096, 2
-    for slot in range(2 * len(HALF)):
-        at = slice(ROWS * slot, ROWS * slot + ROWS)
-        dc, n = divmod(slot, len(HALF))
-        table[:3, at] = np.array((*HALF[n], dc))[:, None]
+    for far, dc, n in np.ndindex(2, 2, FAR):
+        start = DEPTH // 2 * far + ROWS * (FAR * dc + n)
+        at = slice(start, start + ROWS)
+        h = HALF[n + FAR * (1 - far)]
+        table[:3, at] = np.array((*h, dc))[:, None]
         table[3, at] = np.arange(ROWS)
-        table[4, at] = not any(v % 2 for v in HALF[n])
+        table[4, at] = not any(v % 2 for v in h)
     return table
 
 
@@ -211,7 +212,7 @@
     x_hbm, taps_ref, bins_hbm, tw_hbm, fine_hbm, tap_hbm, lag_hbm, geo_hbm,
     out_ref,
     x_ref, tw_ref, fine_ref, tap_ref, lag_ref, geo_ref, lev_ref, pick_ref, hi_ref, lo_ref, lhi_ref, llo_ref,
-    bbuf, abuf, bsend, brecv, codes_ref, wa_ref, hot0, hot1, bmat, s0, s1, x_acc, y_acc, part, r1, r2, r3,
+    bbuf, abuf, bsend, brecv, codes_ref, wa_ref, hot_own, hot0, hot1, bmat, s0, s1, x_acc, y_acc, part, r1, r2, r3,
     in_sem, lev_sem, b_send, b_recv, s_send, s_recv, a_send, a_recv, c_send, c_recv,
     r1_send, r1_recv, r2_send, r2_recv, r3_send, r3_recv,
 ):
@@ -237,7 +238,7 @@
         geo=(geo_hbm, geo_ref), lag=(lag_hbm, lag_ref),
     )
     loads = {name: pltpu.make_async_copy(*refs, in_sem.at[i]) for i, (name, refs) in enumerate(copies.items())}
-    for name in ("geo", "taps", "x", "tw", "fine"):
+    for name in ("x", "tw", "taps", "fine", "geo"):
         loads[name].start()
     for load in lev_loads:
         load.start()
@@ -247,7 +248,9 @@
     plane = [h for h in np.ndindex(4, 4, 2) if any(h)]
     plane.sort(key=lambda h: -(min(h[0], 4 - h[0]) + min(h[1], 4 - h[1])))
     plane = [tuple(map(int, h)) for h in plane]
-    friends = [device(dx, dy, 0, dc) for dx, dy, dc in plane] + [device(0, e, d, 0) for d in (4, 3, 5, 2, 6, 1, 7) for e in (other, 0)]
+    friends = [device(0, e, d, 0) for d in (4, 3, 5) for e in (other, 0)]
+    friends += [device(dx, dy, 0, dc) for dx, dy, dc in plane]
+    friends += [device(0, e, d, 0) for d in (2, 6, 1, 7) for e in (other, 0)]
     barrier = pltpu.get_barrier_semaphore()
     for friend in friends:
         pl.semaphore_signal(barrier, inc=1, device_id=friend, device_id_type=MESH)
@@ -258,25 +261,26 @@
         )
 
     sibling = device(0, 0, 0, 1)
+    white = whiten(x_ref, taps_ref[...], tw_ref, fine_ref, tap_ref, hi_ref, lo_ref, loads)
+    blocks = len(HALF)
+    mine = bbuf.at[0, blocks - 1]
+    mine[...] = fold(jnp.concatenate(white, axis=1), 256)
+
+    pl.semaphore_wait(barrier, len(friends))
+    for n, (dx, dy) in enumerate(HALF[:-1]):
+        remote(mine, bbuf.at[0, n], b_send, b_recv.at[int(n >= FAR)], device(4 - dx, 4 - dy, 0, 0)).start()
+
     loads["geo"].wait()
     dx, dy, dc = (geo_ref[pl.ds(i, 1), :] for i in range(3))
     kind = geo_ref[pl.ds(4, 1), :]
     xx, yy, cc = (x + dx) & 3, (y + dy) & 3, (core + dc) & 1
     source = 24 * (16 * (yy & 1) + 8 * cc + 4 * (yy >> 1) + xx) + geo_ref[pl.ds(3, 1), :]
     pick_ref[...] = (lax.broadcasted_iota(jnp.int32, (LEVEL, DEPTH), 0) == source).astype(F32).astype(BF16)
-    white = whiten(x_ref, taps_ref[...], tw_ref, fine_ref, tap_ref, hi_ref, lo_ref, loads)
-    blocks = len(HALF)
-    mine = bbuf.at[0, blocks - 1]
-    mine[...] = fold(jnp.concatenate(white, axis=1), 256)
-
     order = (1, 7, 2, 6, 3, 5, 4)
     slot_of = {d: n for n, d in enumerate(order)}
     for load in lev_loads:
         load.wait()
     picked = dot(lev_ref[...].reshape(8 * ROWS, LEVEL).astype(F32).astype(BF16), pick_ref[...])
-    pl.semaphore_wait(barrier, len(friends))
-    for n, (dx, dy) in enumerate(HALF[:-1]):
-        remote(mine, bbuf.at[0, n], b_send, b_recv.at[int(n >= FAR)], device(4 - dx, 4 - dy, 0, 0)).start()
     for d in order:
         above = (mod(z + d, 8) > z).astype(jnp.int32)
         keep = jnp.broadcast_to(kind <= above, (ROWS, DEPTH))
@@ -327,7 +331,13 @@
             x_acc[:, lanes] = xs
             y_acc[:, lanes] = ys
 
-    one_hots(hot0, 0, 0)
+    def start(slot, carry):
+        for part in range(2):
+            at = pl.multiple_of(ROWS * NBINS * slot + 12 * NBINS * part, 16)
+            one_hots(hot_own.at[pl.ds(at, 12 * NBINS)], slot, part)
+        return carry
+
+    lax.fori_loop(0, 2, start, 0)
     rows = block_of(mine)
     set_rows(0, rows, 1.0)
     set_rows(1, rows, -1.0)
@@ -338,7 +348,9 @@
     lag_hi, lag_lo = halves(lag_ref[...])
     lhi_ref[...] = lag_hi
     llo_ref[...] = lag_lo
-    bmat[pl.ds(2 * ROWS * blocks, DEPTH - 2 * ROWS * blocks), :] = jnp.zeros((DEPTH - 2 * ROWS * blocks, 384), BF16)
+    for far in range(2):
+        bmat[pl.ds(DEPTH // 2 * far + 240, 16), :] = jnp.zeros((16, 384), BF16)
+
     groups = (pl.ds(FAR, blocks - FAR), pl.ds(0, FAR))
     near = bbuf.at[0, pl.ds(FAR, blocks - 1 - FAR)]
     far = bbuf.at[0, pl.ds(0, FAR)]
@@ -347,49 +359,69 @@
         at = groups[k]
         return remote(bbuf.at[0, at], bbuf.at[1, at], s_send, s_recv.at[k], sibling)
 
-    def assemble(k, first, last):
-        for n in range(first, last, 2):
-            two = [block_of(bbuf.at[k, m]) for m in (n, n + 1)]
-            bmat[pl.ds(ROWS * (blocks * k + n), 2 * ROWS), :] = jnp.concatenate(two, axis=0).astype(BF16)
+    def assemble(far):
+        for i in range(FAR):
+            two = [block_of(bbuf.at[m // FAR, m % FAR + FAR * (1 - far)]) for m in (2 * i, 2 * i + 1)]
+            bmat[pl.ds(DEPTH // 2 * far + 2 * ROWS * i, 2 * ROWS), :] = jnp.concatenate(two, axis=0).astype(BF16)
 
     remote(near, near, b_send, b_recv.at[1], sibling).wait_recv()
     share(0).start()
-    assemble(0, FAR + 1, blocks)
+    share(0).wait_recv()
+    assemble(0)
     remote(far, far, b_send, b_recv.at[0], sibling).wait_recv()
     share(1).start()
-    assemble(0, 0, FAR + 1)
-    share(0).wait_recv()
-    assemble(1, FAR + 1, blocks)
-    share(1).wait_recv()
-    assemble(1, 0, FAR + 1)
+
+    def own_body(step, carry):
+        far, slot = lax.div(step, jnp.int32(2)), mod(step, 2)
+
+        @pl.when(step == 2)
+        def _():
+            share(1).wait_recv()
+            assemble(1)
+
+        @pl.when(step == 3)
+        def _():
+            wait_codes(0)
+            put_codes(0)
+
+        half = pl.ds(pl.multiple_of(DEPTH // 2 * far, 256), DEPTH // 2)
+        at = pl.multiple_of(ROWS * NBINS * slot, 16)
+        s0[...] = dot(hot_own[pl.ds(at, 12 * NBINS), half], bmat[half, :])
+        take(1 - slot, 1, s1)
+        s1[...] = dot(hot_own[pl.ds(at + 12 * NBINS, 12 * NBINS), half], bmat[half, :])
+        one_hots(hot0, 2, 0)
+        take(slot, 0, s0)
+        return carry
+
+    def wait_codes(n):
+        remote(brecv.at[n], brecv.at[n], c_send, c_recv.at[n], sibling).wait_recv()
+
+    def put_codes(n):
+        codes_ref[pl.ds(pl.multiple_of(ROWS * (n + 2), 8), ROWS), :] = unfold(brecv[n], 512, 256)
+
+    lax.fori_loop(0, 4, own_body, 0)
 
     def body(slot, carry):
-        after = slot + 1
-
-        @pl.when((slot > 0) & (slot < 8))
+        @pl.when(slot < 8)
         def _():
-            n = slot - 1
-            remote(brecv.at[n], brecv.at[n], c_send, c_recv.at[n], sibling).wait_recv()
-            codes_ref[pl.ds(pl.multiple_of(ROWS * after, 8), ROWS), :] = unfold(brecv[n], 512, 256)
-
-        @pl.when(slot > 1)
-        def _():
-            n = slot - 2
-            remote(abuf.at[n], abuf.at[n], a_send, a_recv.at[n], sibling).wait_recv()
-            k = lax.div(slot, jnp.int32(2))
-            d = k + mod(slot, 2) * (8 - 2 * k)
-            below = (mod(z + d, 8) < z).astype(F32)
-            set_rows(slot, block_of(abuf.at[n]), 2.0 * below - 1.0)
-
+            wait_codes(slot - 1)
+
+        n, m = slot - 2, jnp.minimum(slot - 1, 6)
+        remote(abuf.at[n], abuf.at[n], a_send, a_recv.at[n], sibling).wait_recv()
         s0[...] = dot(hot0[...], bmat[...])
         one_hots(hot1, slot, 1)
-        take(jnp.maximum(slot - 1, 0), 1, s1)
+        take(slot - 1, 1, s1)
+        put_codes(m)
+        k = lax.div(slot, jnp.int32(2))
+        d = k + mod(slot, 2) * (8 - 2 * k)
+        below = (mod(z + d, 8) < z).astype(F32)
+        set_rows(slot, block_of(abuf.at[n]), 2.0 * below - 1.0)
         s1[...] = dot(hot1[...], bmat[...])
-        one_hots(hot0, jnp.minimum(after, 8), 0)
+        one_hots(hot0, m + 2, 0)
         take(slot, 0, s0)
         return carry
 
-    lax.fori_loop(0, 9, body, 0)
+    lax.fori_loop(2, 9, body, 0)
     take(8, 1, s1)
 
     xs = [x_acc[:, pl.ds(128 * t, 128)] for t in range(3)]
@@ -460,6 +492,7 @@
                 pltpu.VMEM((7, 16, 768), BF16),
                 pltpu.VMEM((9 * ROWS, DEPTH), F32),
                 pltpu.VMEM((9 * ROWS, 768), F32),
+                pltpu.VMEM((2 * ROWS * NBINS, DEPTH), BF16),
                 pltpu.VMEM((12 * NBINS, DEPTH), BF16),
                 pltpu.VMEM((12 * NBINS, DEPTH), BF16),
                 pltpu.VMEM((DEPTH, 384), BF16),

time: 41.8 us -> 41.1 us (0.983)
  Pallas kernels: 40.3 us -> 39.5 us
    pallas_call x1, Pallas kernels: 40.3 us -> 39.5 us  [step(): pl.pallas_call(kernel, out_shape=jax.ShapeDtypeStruct((8, LAGS), F32), in...]
where the time goes in v4:
time: 41.1 us; the launch traced here: 40.9 us
  Pallas kernels  39.5 us (96%)
  local copies, waits for them, and re-layouts  1.32 us (3%)
    pallas_call x1, Pallas kernels, step(): pl.pallas_call(kernel, out_shape=jax.ShapeDtypeStruct((8, LAGS), F32), in...  39.5 us
    unnamed x1, local copies, waits for them, and re-layouts  1.32 us

profile of v4, /device:TPU:1, one launch (start us, length us, event | category | flops | bytes accessed | tf_op | source)
XLA Modules:
  0.0 40.9 jit_solution(17733258401783160718)
XLA Ops:
  0.0 39.5 %stack.1 = f32[8,512]{1,0:T(8,128)} custom-call(f32[24,4096]{1,0:T(8,128)} %x_hbm.1, f32[1,64]{1,0:T(1,128)} %bitcast.1, s32[24,6144]{1,0:T(8,128)} %bins_hbm.1, f32[32,256]{1,0:T(8,128)} %constant.10.clone.tw_hbm, f32[256,256]{1,0:T(8,128)} %constant.11.clone.fine_hbm, f32[64,512]{1,0:T(8,128)} %constant.12.clone.tap_hbm, ...), custom_call_target="tpu_custom_call" | custom-call | tf_op jit(solution)/shard_map/stack/pallas_call | solution.py:475
  39.5 1.3 %copy.10 = f32[8,512]{1,0:T(8,128)} copy(f32[8,512]{1,0:T(8,128)} %stack.1) | data formatting | bytes 32768

commit v5 on v4

--- a/solution.py
+++ b/solution.py
@@ -110,7 +110,15 @@
     win = jnp.where((apart >= -MARGIN) & (apart < MARGIN), 0.5 / MARGIN, 0.0).astype(BF16)
     loads["taps"].wait()
     gains = dot(shifted[:, :TAPS], tap_table[...], precision=lax.Precision.HIGHEST)
+    tail_hi, tail_lo = halves(gains[TAPS:])
+    right_cut = jnp.concatenate([tail_hi, tail_hi, tail_lo, jnp.zeros_like(tail_hi)], axis=0)
     loads["x"].wait()
+    last = x_ref[:, pl.ds(SAMPLES - 128, 128)]
+    last_hi = last.astype(BF16).astype(F32)
+    first_lanes = lax.broadcasted_iota(jnp.int32, (24, 128), 1) < 64
+    moved = pltpu.roll(last_hi, 64, 1)
+    pieces = [jnp.where(first_lanes, moved, last - last_hi), jnp.where(first_lanes, moved, 0.0)]
+    left_cut = jnp.concatenate(pieces, axis=1).astype(BF16)
     loads["tw"].wait()
 
     def body(i, carry):
@@ -152,17 +160,15 @@
                 piece = jnp.concatenate([z[128 * i + at : 128 * i + at + 8, 128 * part : 128 * part + 128] for i in range(3)], 0)
                 tile = jnp.where(lane // 16 == r, piece, tile)
             ext.append(tile)
-    last = jnp.where(lane >= 64, x_ref[:, pl.ds(SAMPLES - 128, 128)], 0.0)
-    cut = dot(last, gains, precision=lax.Precision.HIGHEST)
+    cut = dot(left_cut, right_cut)
     h = [gains[0:1, 128 * k : 128 * k + 128] for k in range(4)]
     re = [h[j] * ext[j] - h[2 + j] * ext[2 + j] - cut[:, 128 * j : 128 * j + 128] for j in range(2)]
     im = [h[j] * ext[2 + j] + h[2 + j] * ext[j] - cut[:, 256 + 128 * j : 384 + 128 * j] for j in range(2)]
     power = jnp.concatenate([re[j] * re[j] + im[j] * im[j] for j in range(2)], axis=1)
-    one = power.astype(BF16)
-    rest = power - one.astype(F32)
-    two = rest.astype(BF16)
-    three = (rest - two.astype(F32)).astype(BF16)
-    smooth = dot(one, win) + dot(two, win) + dot(three, win)
+    one = power.astype(BF16).astype(F32)
+    two = (power - one).astype(BF16).astype(F32)
+    sums = dot(jnp.concatenate([one, two, power - one - two], axis=0).astype(BF16), win)
+    smooth = sums[:24] + sums[24:48] + sums[48:]
     scale = 1.0 / jnp.sqrt(smooth + 1e-06)
     r0, r1 = (re[j] * scale[:, 128 * j : 128 * j + 128] for j in range(2))
     i0, i1 = (im[j] * scale[:, 128 * j : 128 * j + 128] for j in range(2))
@@ -267,8 +273,14 @@
     mine[...] = fold(jnp.concatenate(white, axis=1), 256)
 
     pl.semaphore_wait(barrier, len(friends))
+    order = (1, 7, 2, 6, 3, 5, 4)
+    slot_of = {d: n for n, d in enumerate(order)}
     for n, (dx, dy) in enumerate(HALF[:-1]):
         remote(mine, bbuf.at[0, n], b_send, b_recv.at[int(n >= FAR)], device(4 - dx, 4 - dy, 0, 0)).start()
+
+    for d in order:
+        n = slot_of[8 - d]
+        remote(mine, abuf.at[n], a_send, a_recv.at[n], device(0, 0, d, 0)).start()
 
     loads["geo"].wait()
     dx, dy, dc = (geo_ref[pl.ds(i, 1), :] for i in range(3))
@@ -276,8 +288,6 @@
     xx, yy, cc = (x + dx) & 3, (y + dy) & 3, (core + dc) & 1
     source = 24 * (16 * (yy & 1) + 8 * cc + 4 * (yy >> 1) + xx) + geo_ref[pl.ds(3, 1), :]
     pick_ref[...] = (lax.broadcasted_iota(jnp.int32, (LEVEL, DEPTH), 0) == source).astype(F32).astype(BF16)
-    order = (1, 7, 2, 6, 3, 5, 4)
-    slot_of = {d: n for n, d in enumerate(order)}
     for load in lev_loads:
         load.wait()
     picked = dot(lev_ref[...].reshape(8 * ROWS, LEVEL).astype(F32).astype(BF16), pick_ref[...])
@@ -291,7 +301,6 @@
     for d in order:
         n = slot_of[8 - d]
         remote(bsend.at[d - 1], brecv.at[n], c_send, c_recv.at[n], device(0, 0, d, 0)).start()
-        remote(mine, abuf.at[n], a_send, a_recv.at[n], device(0, 0, d, 0)).start()
 
     def set_rows(slot, rows, sign):
         tiles = [rows[:, 128 * t : 128 * t + 128] for t in range(3)]

time: 41.1 us -> 41.1 us (level)
  no operation moved by 1% of the time
where the time goes in v5:
time: 41.1 us; the launch traced here: 40.9 us
  Pallas kernels  39.6 us (96%)
  local copies, waits for them, and re-layouts  1.32 us (3%)
    pallas_call x1, Pallas kernels, step(): pl.pallas_call(kernel, out_shape=jax.ShapeDtypeStruct((8, LAGS), F32), in...  39.6 us
    unnamed x1, local copies, waits for them, and re-layouts  1.32 us

profile of v5, /device:TPU:1, one launch (start us, length us, event | category | flops | bytes accessed | tf_op | source)
XLA Modules:
  0.0 40.9 jit_solution(8896893899293868092)
XLA Ops:
  0.0 39.6 %stack.1 = f32[8,512]{1,0:T(8,128)} custom-call(f32[24,4096]{1,0:T(8,128)} %x_hbm.1, f32[1,64]{1,0:T(1,128)} %bitcast.1, s32[24,6144]{1,0:T(8,128)} %bins_hbm.1, f32[32,256]{1,0:T(8,128)} %constant.10.clone.tw_hbm, f32[256,256]{1,0:T(8,128)} %constant.11.clone.fine_hbm, f32[64,512]{1,0:T(8,128)} %constant.12.clone.tap_hbm, ...), custom_call_target="tpu_custom_call" | custom-call | tf_op jit(solution)/shard_map/stack/pallas_call | solution.py:484
  39.6 1.3 %copy.10 = f32[8,512]{1,0:T(8,128)} copy(f32[8,512]{1,0:T(8,128)} %stack.1) | data formatting | bytes 32768

commit v6 on v5

--- a/solution.py
+++ b/solution.py
@@ -248,7 +248,6 @@
         loads[name].start()
     for load in lev_loads:
         load.start()
-    loads["lag"].start()
 
     other = 1 - 2 * y_lo
     plane = [h for h in np.ndindex(4, 4, 2) if any(h)]
@@ -282,6 +281,7 @@
         n = slot_of[8 - d]
         remote(mine, abuf.at[n], a_send, a_recv.at[n], device(0, 0, d, 0)).start()
 
+    loads["lag"].start()
     loads["geo"].wait()
     dx, dy, dc = (geo_ref[pl.ds(i, 1), :] for i in range(3))
     kind = geo_ref[pl.ds(4, 1), :]
@@ -375,10 +375,10 @@
 
     remote(near, near, b_send, b_recv.at[1], sibling).wait_recv()
     share(0).start()
+    remote(far, far, b_send, b_recv.at[0], sibling).wait_recv()
+    share(1).start()
     share(0).wait_recv()
     assemble(0)
-    remote(far, far, b_send, b_recv.at[0], sibling).wait_recv()
-    share(1).start()
 
     def own_body(step, carry):
         far, slot = lax.div(step, jnp.int32(2)), mod(step, 2)

time: 41.1 us -> 41.1 us (level)
  no operation moved by 1% of the time
where the time goes in v6:
time: 41.1 us; the launch traced here: 40.9 us
  Pallas kernels  39.6 us (96%)
  local copies, waits for them, and re-layouts  1.32 us (3%)
    pallas_call x1, Pallas kernels, step(): pl.pallas_call(kernel, out_shape=jax.ShapeDtypeStruct((8, LAGS), F32), in...  39.6 us
    unnamed x1, local copies, waits for them, and re-layouts  1.32 us

profile of v6, /device:TPU:1, one launch (start us, length us, event | category | flops | bytes accessed | tf_op | source)
XLA Modules:
  0.0 40.9 jit_solution(14733117220155052327)
XLA Ops:
  0.0 39.6 %stack.1 = f32[8,512]{1,0:T(8,128)} custom-call(f32[24,4096]{1,0:T(8,128)} %x_hbm.1, f32[1,64]{1,0:T(1,128)} %bitcast.1, s32[24,6144]{1,0:T(8,128)} %bins_hbm.1, f32[32,256]{1,0:T(8,128)} %constant.10.clone.tw_hbm, f32[256,256]{1,0:T(8,128)} %constant.11.clone.fine_hbm, f32[64,512]{1,0:T(8,128)} %constant.12.clone.tap_hbm, ...), custom_call_target="tpu_custom_call" | custom-call | tf_op jit(solution)/shard_map/stack/pallas_call | solution.py:484
  39.6 1.3 %copy.10 = f32[8,512]{1,0:T(8,128)} copy(f32[8,512]{1,0:T(8,128)} %stack.1) | data formatting | bytes 32768
